TPU v7x, 32 devices: a whole 2x2x4 slice. The times are simulated.
32 devices in a mesh: groups: 2 (over x), pb: 16 (over z, y, core).
Axes of the slice: x: 2, y: 2, z: 4, core: 2. Of those that a mesh axis runs over, the one named last changes fastest.
Arguments:
- hidden: bfloat16 [8192, 4096], P(('groups', 'pb')), parts along dimension 0, may hold values from -6 to 6
- final_gain: bfloat16 [4096], replicated, may hold values from 0.099609375 to 1.8984375
- last_row: int32 [32, 256], P(('groups', 'pb')), parts along dimension 0, may hold values from 0 to 255, each once within a row
- pair_owner: int32 [4096, 2], P(('groups', 'pb')), parts along dimension 0, may hold values from 0 to 4095, as said below
- hard_negatives: int32 [32, 4], P(('groups', 'pb')), parts along dimension 0, may hold values from -1 to 15, as said below
Outputs:
- pooled_grad: float32 [8192, 4096], P(('groups', 'pb')), parts along dimension 0
- block_loss: float32 [32], P(('groups', 'pb')), parts along dimension 0
There are 2 independent parts, one for each index of `groups`. A program takes and returns all parts, laid end to end along the dimension named above; an argument that names none is the same for every part. Nothing has to cross between parts.
Inputs may be any that keep to these rules, and one draw needn't show every extreme that they name: `last_row`: each device's row names each of its 256 rows once. `pair_owner`: every global sequence index is named exactly once. The 128 pairs of one query block name at most 32 sequences of any one device, and exactly 32 of some device. `hard_negatives`: entry r of query block j is -1 or block (j + r + 1) mod 16. Every row names at least one block, and some row names all 4.
All inputs are finite; a program needn't handle non-finite values.
Results may differ from a plain program's by a relative error of at most 0.006.
Values may be sent and summed in bfloat16 or wider, within the bound.
No kernel may reach another device: no remote copies, remote signals or barrier semaphores. Data moves between devices by JAX's collectives and lax.ppermute only.
A program may use at most 128 MiB of HBM per device.

v0:
```python
import functools

import jax
import jax.numpy as jnp
from jax import lax
from jax.experimental import pallas as pl
from jax.experimental.pallas import tpu as pltpu
from jax.sharding import PartitionSpec as P

inverse_temp = 50.0
token_eps = 1e-05
unit_eps = 1e-06
lanes = 128
bound_steps = 256.0
code_steps = 32000.0
vmem_limit = 56 * 1024 * 1024


def spread(target, at, value):
    count = value.shape[0]
    for half in range(2):
        target[pl.ds(2 * at + half, count, stride=2), :] = value[:, half * lanes : (half + 1) * lanes]


def gathered(source, at, count):
    halves = [source[pl.ds(2 * at + half, count, stride=2), :] for half in range(2)]
    return jnp.concatenate(halves, axis=1)


def row_pair(index):
    return pl.ds(pl.multiple_of(2 * index, 2), 2)


def norm_kernel(
    last_ref, hidden_ref, gain_ref, owner_ref, negative_ref, normed_ref, inv_ref, emb_ref
):
    seqs, width = normed_ref.shape
    parts, _, piece = emb_ref.shape
    pairs = owner_ref.shape[1]
    cuts = [slice(part * piece, (part + 1) * piece) for part in range(parts)]
    sources = lax.broadcasted_iota(jnp.int32, (seqs, seqs), 0)
    pick = jnp.where(sources == last_ref[...], 1.0, 0.0).astype(jnp.bfloat16)

    def folded(squares):
        return functools.reduce(
            jnp.add, [squares[:, at : at + lanes] for at in range(0, piece, lanes)]
        )

    total = jnp.zeros((seqs, lanes), jnp.float32)
    for cut in cuts:
        values = lax.dot_general(
            pick, hidden_ref[:, cut], (((0,), (0,)), ((), ())), preferred_element_type=jnp.float32
        )
        normed_ref[:, cut] = values.astype(jnp.bfloat16)
        total = total + folded(values * values)
    scale = lax.rsqrt(jnp.sum(total, axis=-1, keepdims=True) / width + token_eps)
    total = jnp.zeros((seqs, lanes), jnp.float32)
    for cut in cuts:
        values = normed_ref[:, cut].astype(jnp.float32)
        gain = gain_ref[cut].astype(jnp.float32).reshape(1, piece)
        normed = (values * scale * gain).astype(jnp.bfloat16)
        normed_ref[:, cut] = normed
        pooled = normed.astype(jnp.float32)
        total = total + folded(pooled * pooled)
    inverse = lax.rsqrt(jnp.sum(total, axis=-1, keepdims=True) + unit_eps)
    inv_ref[...] = jnp.broadcast_to(inverse, inv_ref.shape)

    owners = owner_ref[...].astype(jnp.float32)
    high = jnp.floor(owners * (1.0 / 256.0))
    low = owners - 256.0 * high
    row = lax.broadcasted_iota(jnp.int32, (16, pairs), 0)
    spot = lax.broadcasted_iota(jnp.int32, (16, pairs), 1)
    left = jnp.where(row == 0, low[:1], jnp.where(row == 1, high[:1], 0.0))
    right = jnp.where(row == 0, low[1:2], jnp.where(row == 1, high[1:2], 0.0))
    for offset in range(negative_ref.shape[1]):
        named = (negative_ref[0, offset] >= 0).astype(jnp.float32)
        left = jnp.where((row == 2) & (spot == offset), named, left)
    facts = jnp.concatenate([left, right], axis=1).astype(jnp.bfloat16)

    for part, cut in enumerate(cuts):
        emb_ref[part, :seqs] = (normed_ref[:, cut].astype(jnp.float32) * inverse).astype(jnp.bfloat16)
        emb_ref[part, seqs:] = facts


def norm_call(last_row, hidden, gain, owners, hard_negatives, parts):
    seqs, width = hidden.shape
    piece = width // parts
    whole = pl.BlockSpec(memory_space=pltpu.VMEM)
    return pl.pallas_call(
        norm_kernel,
        in_specs=[whole, whole, whole, whole, pl.BlockSpec(memory_space=pltpu.SMEM)],
        out_specs=[whole] * 3,
        out_shape=[
            jax.ShapeDtypeStruct((seqs, width), jnp.bfloat16),
            jax.ShapeDtypeStruct((seqs, lanes), jnp.float32),
            jax.ShapeDtypeStruct((parts, seqs + 16, piece), jnp.bfloat16),
        ],
        compiler_params=pltpu.CompilerParams(vmem_limit_bytes=vmem_limit),
        name="norm_rows",
    )(last_row, hidden, gain, owners, hard_negatives)


def score_kernel(
    blocks,
    pairs,
    window,
    *refs,
):
    emb_ref, q_ref, d_ref, mine_ref, other_ref, top_ref, own_ref, place_ref = refs[:-7]
    wide, picked, tiles, facts, own, named, sems = refs[-7:]
    seqs = emb_ref.shape[1] - 16
    sent = emb_ref[:, seqs:, :].astype(jnp.float32)
    own_ref[...] = (sent[:, 0, :] + 256.0 * sent[:, 1, :]).astype(jnp.int32)
    facts[...] = sent[:, 2, :lanes].astype(jnp.int32)
    fetches = [
        pltpu.make_async_copy(own_ref, own, sems.at[0]),
        pltpu.make_async_copy(facts, named, sems.at[1]),
    ]
    for fetch in fetches:
        fetch.start()

    for part in range(blocks):
        spread(wide, part * seqs, emb_ref[part, :seqs, :].astype(jnp.float32))
    for fetch in fetches:
        fetch.wait()

    def place(block, count):
        place_ref[0, block] = block
        for offset in range(window):
            present = named[block, offset] > 0
            place_ref[offset + 1, block] = jnp.where(present, count, -1)
            count = count + present.astype(jnp.int32)
        return count

    used = lax.fori_loop(0, blocks, place, blocks)
    fine = pairs // blocks

    def clear(spot, carry):
        empty = jnp.zeros((blocks // 2, fine, pairs), jnp.float32)
        at = pl.ds(pl.multiple_of(spot * fine, fine), fine)
        mine_ref[:, at, :] = empty
        other_ref[:, at, :] = empty
        return carry

    lax.fori_loop(used, mine_ref.shape[1] // fine, clear, 0)
    unroll = 32

    def pick_block(block, carry):
        def pick_rows(step, inner):
            base = pl.multiple_of(step * unroll, unroll)
            rows = [wide[row_pair(own[block, base + k]), :] for k in range(unroll)]
            for k in range(unroll):
                picked[row_pair(base + k), :] = rows[k]
            return inner

        lax.fori_loop(0, 2 * pairs // unroll, pick_rows, 0)
        at = pl.multiple_of(block * pairs, pairs)
        q_ref[pl.ds(at, pairs), :] = gathered(picked, 0, pairs).astype(jnp.bfloat16)
        d_ref[pl.ds(at, pairs), :] = gathered(picked, pairs, pairs).astype(jnp.bfloat16)
        return carry

    lax.fori_loop(0, blocks, pick_block, 0)
    d_ref[blocks * pairs :, :] = d_ref[: window * pairs, :]
    even = lax.axis_index("pb") % 2 == 0
    top_ref[...] = jnp.zeros_like(top_ref)

    def score_blocks(step, carry):
        at = pl.multiple_of(step * 2 * pairs, 2 * pairs)
        tiles[...] = inverse_temp * lax.dot_general(
            q_ref[pl.ds(at, 2 * pairs), :],
            d_ref[pl.ds(at, (window + 2) * pairs), :],
            (((1,), (1,)), ((), ())),
            preferred_element_type=jnp.float32,
        )
        for half in range(2):
            for column in range(window + 1):
                spot = place_ref[column, 2 * step + half]

                @pl.when(spot >= 0)
                def _():
                    row = pl.multiple_of(spot * fine, fine)
                    tile = tiles[
                        half * pairs : (half + 1) * pairs,
                        (half + column) * pairs : (half + column + 1) * pairs,
                    ]
                    parted = tile.reshape(blocks // 2, 2, fine, pairs)
                    first, second = parted[:, 0], parted[:, 1]
                    mine_ref[:, pl.ds(row, fine), :] = jnp.where(even, first, second)
                    other_ref[:, pl.ds(row, fine), :] = jnp.where(even, second, first)
                    size = jnp.maximum(jnp.abs(first), jnp.abs(second))
                    top_ref[...] = jnp.maximum(top_ref[...], jnp.max(size, axis=0))

        return carry

    lax.fori_loop(0, blocks // 2, score_blocks, 0)


def score_call(embedded, room, blocks, pairs, window):
    _, rows, piece = embedded.shape
    fine = pairs // blocks
    whole = pl.BlockSpec(memory_space=pltpu.VMEM)
    scalars = pl.BlockSpec(memory_space=pltpu.SMEM)
    return pl.pallas_call(
        functools.partial(score_kernel, blocks, pairs, window),
        in_specs=[whole],
        out_specs=[whole, whole, whole, whole, whole, whole, scalars],
        out_shape=[
            jax.ShapeDtypeStruct((blocks * pairs, piece), jnp.bfloat16),
            jax.ShapeDtypeStruct(((blocks + window) * pairs, piece), jnp.bfloat16),
            jax.ShapeDtypeStruct((blocks // 2, room * fine, pairs), jnp.float32),
            jax.ShapeDtypeStruct((blocks // 2, room * fine, pairs), jnp.float32),
            jax.ShapeDtypeStruct((fine, pairs), jnp.float32),
            jax.ShapeDtypeStruct((blocks, 2 * pairs), jnp.int32),
            jax.ShapeDtypeStruct((window + 1, blocks), jnp.int32),
        ],
        scratch_shapes=[
            pltpu.VMEM((2 * blocks * (rows - 16), lanes), jnp.float32),
            pltpu.VMEM((4 * pairs, lanes), jnp.float32),
            pltpu.VMEM((2 * pairs, (window + 2) * pairs), jnp.float32),
            pltpu.VMEM((blocks, lanes), jnp.int32),
            pltpu.SMEM((blocks, 2 * pairs), jnp.int32),
            pltpu.SMEM((blocks, lanes), jnp.int32),
            pltpu.SemaphoreType.DMA((2,)),
        ],
        compiler_params=pltpu.CompilerParams(vmem_limit_bytes=vmem_limit),
        name="partial_scores",
    )(embedded)


def merge_kernel(mine_ref, other_ref, top_ref, other_top_ref, own_ref, *code_refs):
    chips, rows, pairs = mine_ref.shape
    steps = code_refs[0].shape[0] - 1
    fine = rows // steps // 2
    chip = lax.axis_index("pb") // 2

    def highest(ref):
        return jnp.max(jnp.max(ref[...], axis=1, keepdims=True), axis=0, keepdims=True)

    top = highest(top_ref) + highest(other_top_ref)
    bound = jnp.ceil(top * bound_steps) + 1.0
    scale = code_steps * bound_steps / bound
    own_ref[...] = mine_ref[chip] + other_ref[chip]
    for hop, code_ref in enumerate(code_refs):
        target = chip ^ (hop + 1)

        def encode(step, carry):
            at = pl.multiple_of(step * 2 * fine, 2 * fine)
            there = pl.ds(at, 2 * fine)
            codes = jnp.round((mine_ref[target, there, :] + other_ref[target, there, :]) * scale)
            code_ref[step] = codes.astype(jnp.int32).astype(jnp.int16)
            return carry

        lax.fori_loop(0, steps, encode, 0)
        code_ref[steps] = jnp.broadcast_to(bound, (2 * fine, pairs)).astype(jnp.int32).astype(jnp.int16)


def merge_call(mine, other, top, other_top, blocks):
    chips, rows, pairs = mine.shape
    fine = pairs // blocks
    whole = pl.BlockSpec(memory_space=pltpu.VMEM)
    coded = jax.ShapeDtypeStruct((rows // (2 * fine) + 1, 2 * fine, pairs), jnp.int16)
    return pl.pallas_call(
        merge_kernel,
        in_specs=[whole] * 4,
        out_specs=[whole] * chips,
        out_shape=[jax.ShapeDtypeStruct((rows, pairs), jnp.float32)] + [coded] * (chips - 1),
        compiler_params=pltpu.CompilerParams(vmem_limit_bytes=vmem_limit),
        name="merge_scores",
    )(mine, other, top, other_top)


def softmax_kernel(blocks, window, place_ref, own_ref, *refs):
    code_refs, (c_ref, packed, masked) = refs[:-3], refs[-3:]
    room, fine, pairs = packed.shape
    count = blocks * fine
    unit = 1.0 / (code_steps * bound_steps)
    scales = [ref[room // 2].astype(jnp.int32).astype(jnp.float32) * unit for ref in code_refs]

    def decode(step, carry):
        both = own_ref[pl.ds(pl.multiple_of(step * 2 * fine, 2 * fine), 2 * fine), :]
        for ref, scale in zip(code_refs, scales):
            both = both + ref[step].astype(jnp.int32).astype(jnp.float32) * scale
        packed[2 * step] = both[:fine]
        packed[2 * step + 1] = both[fine:]
        return carry

    lax.fori_loop(0, room // 2, decode, 0)
    for block in range(blocks):
        for column in range(window + 1):
            spot = place_ref[column, block]
            tile = packed[jnp.maximum(spot, 0)]
            masked[block * fine : (block + 1) * fine, column * pairs : (column + 1) * pairs] = (
                jnp.where(spot >= 0, tile, -jnp.inf)
            )
    row = lax.broadcasted_iota(jnp.int32, (count, pairs), 0)
    lane = lax.broadcasted_iota(jnp.int32, (count, pairs), 1)
    target = lane == lax.axis_index("pb") * fine + row % fine
    pieces = [masked[:, column * pairs : (column + 1) * pairs] for column in range(window + 1)]
    row_max = jnp.max(functools.reduce(jnp.maximum, pieces), axis=1, keepdims=True)
    total = functools.reduce(jnp.add, [jnp.exp(piece - row_max) for piece in pieces])
    log_total = row_max + jnp.log(jnp.sum(total, axis=1, keepdims=True))
    positive = jnp.sum(jnp.where(target, pieces[0], 0.0), axis=1, keepdims=True)
    for column, piece in enumerate(pieces):
        share = jnp.exp(piece - log_total)
        if column == 0:
            share = share - jnp.where(target, 1.0, 0.0)
        masked[:, column * pairs : (column + 1) * pairs] = inverse_temp * share
    for block in range(blocks):
        for column in range(window + 1):
            spot = place_ref[column, block]

            @pl.when(spot >= 0)
            def _():
                packed[spot] = masked[
                    block * fine : (block + 1) * fine, column * pairs : (column + 1) * pairs
                ]

    for step in range(room // 2):
        both = jnp.concatenate([packed[2 * step], packed[2 * step + 1]], axis=0)
        c_ref[step] = both.astype(jnp.bfloat16)
    losses = jnp.sum(
        jnp.where(lane == row // fine, log_total - positive, 0.0), axis=0, keepdims=True
    )
    coarse = losses.astype(jnp.bfloat16).astype(jnp.float32)
    rank = lax.broadcasted_iota(jnp.int32, (2 * fine, pairs), 0)
    both = jnp.where(rank == 0, coarse, jnp.where(rank == 1, losses - coarse, 0.0))
    c_ref[room // 2] = both.astype(jnp.bfloat16)


def softmax_call(place, own_scores, codes, blocks, window):
    steps, fine, pairs = codes[0].shape
    room, fine = 2 * (steps - 1), fine // 2
    whole = pl.BlockSpec(memory_space=pltpu.VMEM)
    return pl.pallas_call(
        functools.partial(softmax_kernel, blocks, window),
        in_specs=[pl.BlockSpec(memory_space=pltpu.SMEM), whole] + [whole] * len(codes),
        out_specs=whole,
        out_shape=jax.ShapeDtypeStruct((room // 2 + 1, 2 * fine, pairs), jnp.bfloat16),
        scratch_shapes=[
            pltpu.VMEM((room, fine, pairs), jnp.float32),
            pltpu.VMEM((blocks * fine, (window + 1) * pairs), jnp.float32),
        ],
        compiler_params=pltpu.CompilerParams(vmem_limit_bytes=vmem_limit),
        name="softmax_rows",
    )(place, own_scores, *codes)


def grad_kernel(
    blocks,
    pairs,
    window,
    own_ref,
    place_ref,
    q_ref,
    d_ref,
    *refs,
):
    part_refs = refs[:-7]
    out_ref, loss_ref, wide, dsum, picked, packed, square = refs[-7:]
    fine = pairs // blocks
    room = packed.shape[1]
    me = lax.axis_index("pb")
    masks = swap_masks(blocks)
    unroll = 32
    losses = 0.0
    for part in part_refs:
        sent = part[:, room // 2].astype(jnp.float32)
        losses = losses + jnp.sum(sent[:, 0, :] + sent[:, 1, :], axis=0, keepdims=True) / pairs
    lane = lax.broadcasted_iota(jnp.int32, losses.shape, 1)
    mine = jnp.where(lane == me, losses, 0.0)
    loss_ref[...] = jnp.broadcast_to(jnp.sum(mine, axis=1, keepdims=True), loss_ref.shape)
    dsum[...] = jnp.zeros_like(dsum)
    square[...] = jnp.zeros_like(square)

    def unpack(step, carry):
        for part, mask in zip(part_refs, masks):
            both = part[:, step].astype(jnp.float32)
            for at, apart in enumerate(mask):
                packed[me ^ apart, 2 * step] = both[at, :fine]
                packed[me ^ apart, 2 * step + 1] = both[at, fine:]
        return carry

    lax.fori_loop(0, room // 2, unpack, 0)

    def scatter_rows(block, offset, start):
        def step_rows(step, inner):
            base = pl.multiple_of(step * unroll, unroll)
            rows = [picked[row_pair(start + base + k), :] for k in range(unroll)]
            for k in range(unroll):
                wide[row_pair(own_ref[block, offset + base + k]), :] = rows[k]
            return inner

        lax.fori_loop(0, pairs // unroll, step_rows, 0)

    def two_blocks(step, carry):
        for half in range(2):
            for column in range(window + 1):
                spot = place_ref[column, 2 * step + half]
                tile = packed[:, jnp.maximum(spot, 0)].reshape(pairs, pairs)
                square[
                    half * pairs : (half + 1) * pairs,
                    (half + column) * pairs : (half + column + 1) * pairs,
                ] = jnp.where(spot >= 0, tile, 0.0).astype(jnp.bfloat16)
        at = pl.multiple_of(step * 2 * pairs, 2 * pairs)
        there = pl.ds(at, (window + 2) * pairs)
        coefficients = square[...]
        summed = jnp.dot(coefficients, d_ref[there, :], preferred_element_type=jnp.float32)
        spread(picked, 0, summed)
        dsum[there, :] += lax.dot_general(
            coefficients,
            q_ref[pl.ds(at, 2 * pairs), :],
            (((0,), (0,)), ((), ())),
            preferred_element_type=jnp.float32,
        )
        for half in range(2):
            scatter_rows(2 * step + half, 0, half * pairs)
        return carry

    lax.fori_loop(0, blocks // 2, two_blocks, 0)
    dsum[: window * pairs, :] += dsum[blocks * pairs :, :]

    def doc_block(block, carry):
        at = pl.multiple_of(block * pairs, pairs)
        spread(picked, 0, dsum[pl.ds(at, pairs), :])
        scatter_rows(block, pairs, 0)
        return carry

    lax.fori_loop(0, blocks, doc_block, 0)
    slots = out_ref.shape[1]
    for part in range(blocks):
        out_ref[part] = gathered(wide, part * slots, slots).astype(jnp.bfloat16)


def grad_call(own, place, parts, queries, documents, blocks, pairs, window):
    count, piece = queries.shape
    seqs = 2 * count
    room = 2 * (parts[0].shape[1] - 1)
    whole = pl.BlockSpec(memory_space=pltpu.VMEM)
    scalars = pl.BlockSpec(memory_space=pltpu.SMEM)
    return pl.pallas_call(
        functools.partial(grad_kernel, blocks, pairs, window),
        in_specs=[scalars, scalars, whole, whole] + [whole] * len(parts),
        out_specs=[whole, whole],
        out_shape=[
            jax.ShapeDtypeStruct((blocks, seqs // blocks, piece), jnp.bfloat16),
            jax.ShapeDtypeStruct((1, lanes), jnp.float32),
        ],
        scratch_shapes=[
            pltpu.VMEM((2 * seqs, lanes), jnp.float32),
            pltpu.VMEM(((blocks + window) * pairs, piece), jnp.float32),
            pltpu.VMEM((4 * pairs, lanes), jnp.float32),
            pltpu.VMEM((blocks, room, pairs // blocks, pairs), jnp.float32),
            pltpu.VMEM((2 * pairs, (window + 2) * pairs), jnp.bfloat16),
        ],
        compiler_params=pltpu.CompilerParams(vmem_limit_bytes=vmem_limit),
        name="slice_grads",
    )(own, place, queries, documents, *parts)


def project_kernel(grad_ref, normed_ref, inv_ref, out_ref):
    parts, _, piece = grad_ref.shape
    cuts = [slice(part * piece, (part + 1) * piece) for part in range(parts)]
    inverse = inv_ref[:, :1]
    total = 0.0
    for part, cut in enumerate(cuts):
        unit = normed_ref[:, cut].astype(jnp.float32) * inverse
        total = total + unit * grad_ref[part].astype(jnp.float32)
    along = jnp.sum(total, axis=-1, keepdims=True)
    for part, cut in enumerate(cuts):
        unit = normed_ref[:, cut].astype(jnp.float32) * inverse
        out_ref[:, cut] = grad_ref[part].astype(jnp.float32) - unit * along


def project_call(returned, normed, inverse):
    parts, seqs, piece = returned.shape
    width = normed.shape[1]
    rows = 64
    return pl.pallas_call(
        project_kernel,
        grid=(seqs // rows,),
        in_specs=[
            pl.BlockSpec((parts, rows, piece), lambda i: (0, i, 0)),
            pl.BlockSpec((rows, width), lambda i: (i, 0)),
            pl.BlockSpec((rows, lanes), lambda i: (i, 0)),
        ],
        out_specs=pl.BlockSpec((rows, width), lambda i: (i, 0)),
        out_shape=jax.ShapeDtypeStruct((seqs, width), jnp.float32),
        compiler_params=pltpu.CompilerParams(vmem_limit_bytes=vmem_limit),
        name="project_out",
    )(returned, normed, inverse)


def swapped(value, apart):
    pairs = [(at, at ^ apart) for at in range(lax.axis_size("pb"))]
    return lax.ppermute(value, "pb", pairs)


def swap_bits(devices):
    bits = [1 << bit for bit in reversed(range(devices.bit_length() - 1))]
    return bits[:-2], bits[-2], bits[-1]


def swap_masks(devices):
    far, side, last = swap_bits(devices)
    held = [0]
    for apart in far:
        held = held + [mask ^ apart for mask in held]
    held = held + [mask ^ side for mask in held]
    return [held, [mask ^ last for mask in held]]


def gather_all(value):
    far, side, last = swap_bits(lax.axis_size("pb"))
    held = value[None]
    beside = [swapped(held, side)]
    for apart in far:
        arrived = swapped(held, apart)
        beside.append(swapped(arrived, side))
        held = jnp.concatenate([held, arrived], axis=0)
    held = jnp.concatenate([held] + beside, axis=0)
    return [held, swapped(held, last)]


def middle(embedded, room, devices, pairs, window):
    queries, documents, mine, other, top, own, place = score_call(
        embedded, room, devices, pairs, window
    )
    own_scores, *codes = merge_call(mine, swapped(other, 1), top, swapped(top, 1), devices)
    codes = [swapped(code, 2 * (hop + 1)) for hop, code in enumerate(codes)]
    parts = gather_all(softmax_call(place, own_scores, codes, devices, window))
    grads, loss = grad_call(own, place, parts, queries, documents, devices, pairs, window)
    return grads, loss[0, :1]


def feature_plan(hidden, final_gain, last_row, pair_owner, hard_negatives):
    devices = lax.axis_size("pb")
    seqs, width = hidden.shape
    pairs = pair_owner.shape[0]
    window = hard_negatives.shape[1]
    normed, inverse, embedding = norm_call(
        last_row, hidden, final_gain, pair_owner.T, hard_negatives, devices
    )
    embedded = lax.all_to_all(embedding, "pb", split_axis=0, concat_axis=0, tiled=True)
    most = devices * (window + 1)
    rooms = [most * part // 20 for part in (10, 11, 12, 13, 14, 16, 20)]
    used = devices + jnp.sum(embedded[:, seqs + 2, :window].astype(jnp.float32))
    level = sum((used > room).astype(jnp.int32) for room in rooms[:-1])
    grads, loss = lax.switch(
        level,
        [
            functools.partial(middle, room=room, devices=devices, pairs=pairs, window=window)
            for room in rooms
        ],
        embedded,
    )
    returned = lax.all_to_all(grads, "pb", split_axis=0, concat_axis=0, tiled=True)
    return project_call(returned, normed, inverse), loss


def from_behind(value, axis, steps):
    count = lax.axis_size(axis)
    pairs = [(source, (source + steps) % count) for source in range(count)]
    return lax.ppermute(value, axis, pairs)


def similarity(queries, documents):
    return inverse_temp * lax.dot_general(
        queries, documents, (((1,), (1,)), ((), ())), preferred_element_type=jnp.float32
    )


def transposed(weights, queries):
    return lax.dot_general(
        weights, queries, (((0,), (0,)), ((), ())), preferred_element_type=jnp.float32
    )


def combine_docs(weights, documents):
    return jnp.dot(weights, documents, preferred_element_type=jnp.float32)


def skipped(listed, function, operands, out_shape):
    return lax.cond(
        listed,
        lambda inputs: function(*inputs),
        lambda inputs: jnp.zeros(out_shape, jnp.float32),
        operands,
    )


def row_plan(hidden, final_gain, last_row, pair_owner, hard_negatives):
    values = hidden.astype(jnp.float32)
    scale_row = lax.rsqrt(jnp.mean(values * values, axis=-1, keepdims=True) + token_eps)
    normed = (values * scale_row * final_gain.astype(jnp.float32)).astype(jnp.bfloat16)
    seq_count = last_row.shape[1]
    model_width = hidden.shape[1]
    pooled = normed[last_row[0]].astype(jnp.float32)
    inverse_norm = lax.rsqrt(jnp.sum(pooled * pooled, axis=-1, keepdims=True) + 1e-06)
    unit_vec = pooled * inverse_norm
    embedding = unit_vec.astype(jnp.bfloat16)
    devices = lax.axis_size("pb")
    capacity = 2 * seq_count // devices
    pair_count = pair_owner.shape[0]
    wanted = jnp.concatenate([pair_owner[:, 0], pair_owner[:, 1]])
    holder = wanted // seq_count
    within = wanted % seq_count
    entry_ids = jnp.arange(2 * pair_count, dtype=jnp.int32)
    earlier = (holder[None, :] == holder[:, None]) & (entry_ids[None, :] < entry_ids[:, None])
    position = jnp.sum(earlier.astype(jnp.int32), axis=1)
    request = jnp.full((devices, capacity), -1, jnp.int32).at[holder, position].set(within)
    served = lax.all_to_all(request, "pb", split_axis=0, concat_axis=0, tiled=True)
    outgoing = jnp.where(
        served[:, :, None] >= 0, embedding[jnp.maximum(served, 0)], jnp.zeros((), jnp.bfloat16)
    )
    received = lax.all_to_all(outgoing, "pb", split_axis=0, concat_axis=0, tiled=True)
    gathered = received[holder, position]
    queries = gathered[:pair_count]
    own_docs = gathered[pair_count:]
    listed_ids = hard_negatives[0]
    window = hard_negatives.shape[1]
    listed = [listed_ids[offset] >= 0 for offset in range(window)]
    neighbours = []
    moving = own_docs
    for offset in range(window):
        moving = from_behind(moving, "pb", -1)
        neighbours.append(moving)
    tile_shape = (pair_count, pair_count)
    score_blocks = [similarity(queries, own_docs)]
    for offset in range(window):
        score_blocks.append(
            skipped(listed[offset], similarity, (queries, neighbours[offset]), tile_shape)
        )
    all_scores = jnp.concatenate(score_blocks, axis=1)
    usable = jnp.concatenate(
        [jnp.ones((pair_count,), jnp.bool_)]
        + [jnp.broadcast_to(listed[offset], (pair_count,)) for offset in range(window)]
    )
    masked = jnp.where(usable[None, :], all_scores, -jnp.inf)
    row_max = jnp.max(masked, axis=1, keepdims=True)
    log_total = row_max + jnp.log(jnp.sum(jnp.exp(masked - row_max), axis=1, keepdims=True))
    diagonal = jnp.arange(pair_count, dtype=jnp.int32)
    positive = all_scores[diagonal, diagonal]
    block_loss = jnp.mean(log_total[:, 0] - positive).reshape(1)
    columns = jnp.arange((window + 1) * pair_count, dtype=jnp.int32)
    target = (columns[None, :] == diagonal[:, None]).astype(jnp.float32)
    coefficients = (inverse_temp * (jnp.exp(masked - log_total) - target)).astype(jnp.bfloat16)
    pieces = [
        coefficients[:, offset * pair_count : (offset + 1) * pair_count]
        for offset in range(window + 1)
    ]
    grad_shape = (pair_count, model_width)
    query_sum = combine_docs(pieces[0], own_docs)
    for offset in range(window):
        query_sum = query_sum + skipped(
            listed[offset], combine_docs, (pieces[offset + 1], neighbours[offset]), grad_shape
        )
    query_grad = query_sum.astype(jnp.bfloat16)
    own_part = transposed(pieces[0], queries).astype(jnp.bfloat16)
    partial_value = [
        skipped(listed[offset], transposed, (pieces[offset + 1], queries), grad_shape).astype(
            jnp.bfloat16
        )
        for offset in range(window)
    ]
    running = partial_value[window - 1].astype(jnp.float32)
    for offset in range(window):
        running = from_behind(running, "pb", 1)
        if offset + 1 < window:
            running = running + partial_value[window - 2 - offset].astype(jnp.float32)
    doc_grad = (own_part.astype(jnp.float32) + running).astype(jnp.bfloat16)
    answers = jnp.concatenate([query_grad, doc_grad], axis=0)
    returning = (
        jnp.zeros((devices, capacity, model_width), jnp.bfloat16).at[holder, position].set(answers)
    )
    returned = lax.all_to_all(returning, "pb", split_axis=0, concat_axis=0, tiled=True)
    slot_ids = jnp.where(served >= 0, served, seq_count).reshape(-1)
    emb_grad = (
        jnp.zeros((seq_count, model_width), jnp.bfloat16)
        .at[slot_ids]
        .set(returned.reshape(-1, model_width), mode="drop")
    )
    gradient = emb_grad.astype(jnp.float32)
    pooled_grad = gradient - unit_vec * jnp.sum(unit_vec * gradient, axis=-1, keepdims=True)
    return (pooled_grad, block_loss)


def solution(mesh):
    def local(hidden, final_gain, last_row, pair_owner, hard_negatives):
        plan = feature_plan if hidden.shape[1] >= lanes * mesh.shape["pb"] else row_plan
        return plan(hidden, final_gain, last_row, pair_owner, hard_negatives)

    return jax.shard_map(
        local,
        mesh=mesh,
        in_specs=(
            P(("groups", "pb"), None),
            P(),
            P(("groups", "pb"), None),
            P(("groups", "pb"), None),
            P(("groups", "pb"), None),
        ),
        out_specs=(P(("groups", "pb"), None), P(("groups", "pb"))),
        check_vma=False,
    )
```

profile of v0, /device:TPU:1, one launch (start us, length us, event | category | flops | bytes accessed | tf_op | source)
XLA Modules:
  0.0 221.2 jit_solution(12389887688885492699)
XLA Ops:
  0.6 5.7 %norm_rows.1 = (bf16[256,4096]{1,0:T(8,128)(2,1)}, f32[256,128]{1,0:T(8,128)}, bf16[16,272,256]{2,1,0:T(8,128)(2,1)}) custom-call(s32[1,256]{1,0:T(1,128)} %last_ref.1, bf16[256,4096]{1,0:T(8,128)(2,1)} %hidden_ref.1, bf16[4096]{0:T(1024)(128)(2,1)} %gain_ref.1, s32[2,128]{1,0:T(2,128)} %bitcast.50, s32[1,4]{1,0:T(1,128)} %negative_ref.1), custom_call_target="tpu_custom_call" | custom-call | tf_op jit(solution)/shard_map/norm_rows/pallas_call | solution.py:89
  6.3 59.2 %all_to_all.31 = bf16[16,272,256]{2,1,0:T(8,128)(2,1)S(1)} all-to-all(bf16[16,272,256]{2,1,0:T(8,128)(2,1)} %get-tuple-element.133), channel_id=1, replica_groups=mesh['groups'=2,'pb'=16] {'pb'}, dimensions={0} | all-to-all | bytes 4456448 | tf_op jit(solution)/shard_map/all_to_all | solution.py:543
  65.5 0.6 fusion
  66.8 97.8 %conditional.1 = (bf16[16,256,256]{2,1,0:T(8,128)(2,1)S(1)}, f32[1]{0:T(128)}) conditional(s32[]{:T(128)} %clamp.3, bf16[16,272,256]{2,1,0:T(8,128)(2,1)S(1)} %all_to_all.31, bf16[16,272,256]{2,1,0:T(8,128)(2,1)S(1)} %all_to_all.31, bf16[16,272,256]{2,1,0:T(8,128)(2,1)S(1)} %all_to_all.31, ...), branch_computations={%region_1.0_spmd, %region_2.0_spmd, %region_3.0_spmd, %region_4.0_... | conditional | flops 167936 | bytes 54592412 | solution.py:548
  67.0 19.1 %partial_scores.9 = (bf16[2048,256]{1,0:T(8,128)(2,1)}, bf16[2560,256]{1,0:T(8,128)(2,1)}, f32[8,384,128]{2,1,0:T(8,128)}, f32[8,384,128]{2,1,0:T(8,128)}, f32[8...) custom-call(bf16[16,272,256]{2,1,0:T(8,128)(2,1)S(1)} %refs_0_.2), custom_call_target="tpu_custom_call" | custom-call | tf_op jit(solution)/shard_map/cond/branch_2_fun/partial_scores/pallas_call | solution.py:203
  86.7 3.1 %collective-permute-done.31.other_top_ref = f32[8,128]{1,0:T(8,128)S(1)} collective-permute-done((f32[8,128]{1,0:T(8,128)}, f32[8,128]{1,0:T(8,128)S(1)}, u32[]{:S(2)}, u32[]{:S(2)}) %collective-permute-start.31) | collective-permute-done | bytes 4128 | tf_op jit(solution)/shard_map/cond/branch_2_fun/ppermute | solution.py:495
  89.8 0.6 copy-done.72
  90.9 4.2 %merge_scores.9 = (f32[384,128]{1,0:T(8,128)}, s16[25,16,128]{2,1,0:T(8,128)(2,1)}, s16[25,16,128]{2,1,0:T(8,128)(2,1)}, s16[25,16,128]{2,1,0:T(8,128)(2,1)}, s1...) custom-call(f32[8,384,128]{2,1,0:T(8,128)} %get-tuple-element.45.min, ...), custom_call_target="tpu_custom_call" | custom-call | tf_op jit(solution)/shard_map/cond/branch_2_fun/merge_scores/pallas_call | solution.py:262
  96.0 1.8 collective-permute-start.34
  97.8 0.8 collective-permute-start.35
  98.6 1.6 collective-permute-start.36
  100.3 1.5 collective-permute-start.37
  101.8 2.6 %collective-permute-start.38 = (s16[25,16,128]{2,1,0:T(8,128)(2,1)}, s16[25,16,128]{2,1,0:T(8,128)(2,1)S(1)}, u32[]{:S(2)}, u32[]{:S(2)}) collective-permute-start(s16[25,16,128]{2,1,0:T(8,128)(2,1)} %get-tuple-element.55), channel_id=1, source_target_pairs={{0,14},{1,15},{2,12},{3,13},{4,10},{5,11},{6,8},{7,9},{8,6},{9,7},... | collective-permute-start | bytes 307208 | tf_op jit(solution)/shard_map/cond/branch_2_fun/ppermute | solution.py:495
  104.4 9.8 %collective-permute-done.36.refs_4_ = s16[25,16,128]{2,1,0:T(8,128)(2,1)S(1)} collective-permute-done((s16[25,16,128]{2,1,0:T(8,128)(2,1)}, s16[25,16,128]{2,1,0:T(8,128)(2,1)S(1)}, u32[]{:S(2)}, u32[]{:S(2)}) %collective-permute-start.36) | collective-permute-done | bytes 102432 | tf_op jit(solution)/shard_map/cond/branch_2_fun/ppermute | solution.py:495
  114.3 0.6 copy-done.53
  114.9 3.2 %softmax_rows.9 = bf16[25,16,128]{2,1,0:T(8,128)(2,1)} custom-call(s32[5,16]{1,0:T(8,128)} %get-tuple-element.42.place_ref, f32[384,128]{1,0:T(8,128)} %get-tuple-element.48.own_ref, s16[25,16,128]{2,1,0:T(8,128)(2,1)} %copy-done.49, s16[25,16,128]{2,1,0:T(8,128)(2,1)} %copy-done.50, s16[25,16,128]{2,1,0:T(8,128)(2,1)} %copy-done.51, ...), custom_call_target="tpu_custom_call" | custom-call | tf_op jit(solution)/shard_map/cond/branch_2_fun/softmax_rows/pallas_call | solution.py:334
  118.1 5.1 %collective-permute-start.39 = (bf16[1,25,16,128]{3,2,1,0:T(8,128)(2,1)}, bf16[1,25,16,128]{3,2,1,0:T(8,128)(2,1)S(1)}, u32[]{:S(2)}, u32[]{:S(2)}) collective-permute-start(bf16[1,25,16,128]{3,2,1,0:T(8,128)(2,1)} %bitcast.41), channel_id=1, source_target_pairs={{0,8},{1,9},{2,10},{3,11},{4,12},{5,13},{6,14},{7,15},{8,0},{9,1},... | collective-permute-start | bytes 307208 | tf_op jit(solution)/shard_map/cond/branch_2_fun/ppermute | solution.py:495
  123.3 2.3 %collective-permute-done.39 = bf16[1,25,16,128]{3,2,1,0:T(8,128)(2,1)S(1)} collective-permute-done((bf16[1,25,16,128]{3,2,1,0:T(8,128)(2,1)}, bf16[1,25,16,128]{3,2,1,0:T(8,128)(2,1)S(1)}, u32[]{:S(2)}, u32[]{:S(2)}) %collective-permute-start.39) | collective-permute-done | bytes 102432 | tf_op jit(solution)/shard_map/cond/branch_2_fun/ppermute | solution.py:495
  125.5 0.9 pad_maximum_fusion.2
  126.4 2.0 collective-permute-start.40
  128.4 0.9 constant_dynamic-update-slice_fusion.17
  129.7 1.1 collective-permute-start.42
  130.8 0.8 collective-permute-done.40
  132.0 1.0 collective-permute-done.41
  133.1 1.4 collective-permute-done.42
  134.4 3.1 %collective-permute-done.43 = bf16[2,25,16,128]{3,2,1,0:T(8,128)(2,1)S(1)} collective-permute-done((bf16[2,25,16,128]{3,2,1,0:T(8,128)(2,1)S(1)}, bf16[2,25,16,128]{3,2,1,0:T(8,128)(2,1)S(1)}, u32[]{:S(2)}, u32[]{:S(2)}) %collective-permute-start.43) | collective-permute-done | bytes 204832 | tf_op jit(solution)/shard_map/cond/branch_2_fun/ppermute | solution.py:495
  137.6 4.9 %collective-permute-start.44 = (bf16[8,25,16,128]{3,2,1,0:T(8,128)(2,1)S(1)}, bf16[8,25,16,128]{3,2,1,0:T(8,128)(2,1)S(1)}, u32[]{:S(2)}, u32[]{:S(2)}) collective-permute-start(bf16[8,25,16,128]{3,2,1,0:T(8,128)(2,1)S(1)} %constant_dynamic-update-slice_fusion.12.refs_0_), channel_id=1, source_target_pairs={{0,1},{1,0},{2,3},{3,2},{4,5},{5,4},{6,7},{7,6},{8,9},{9,8},{10,11... | collective-permute-start | bytes 2457608 | tf_op jit(solution)/shard_map/cond/branch_2_fun/ppermute | solution.py:495
  142.5 2.0 collective-permute-done.44.refs_1_
  144.5 0.9 copy-done.18
  145.4 18.9 %slice_grads.9 = (bf16[16,256,256]{2,1,0:T(8,128)(2,1)S(1)}, f32[1,128]{1,0:T(1,128)}) custom-call(s32[16,256]{1,0:T(8,128)} %get-tuple-element.41.own_ref, s32[5,16]{1,0:T(8,128)} %get-tuple-element.42.place_ref, bf16[2048,256]{1,0:T(8,128)(2,1)} %get-tuple-element.43.q_ref, bf16[2560,256]{1,0:T(8,128)(2,1)} %get-tuple-element.44.d_ref, ...), custom_call_target="tpu_custom_call" | custom-call | tf_op jit(solution)/shard_map/cond/branch_2_fun/slice_grads/pallas_call | solution.py:440
  164.6 51.2 %all_to_all.32.grad_ref = bf16[16,256,256]{2,1,0:T(8,128)(2,1)} all-to-all(bf16[16,256,256]{2,1,0:T(8,128)(2,1)S(1)} %get-tuple-element.134), channel_id=1, replica_groups=mesh['groups'=2,'pb'=16] {'pb'}, dimensions={0} | all-to-all | bytes 4194304 | tf_op jit(solution)/shard_map/all_to_all | solution.py:556
  215.8 5.4 %project_out.1 = f32[256,4096]{1,0:T(8,128)} custom-call(bf16[16,256,256]{2,1,0:T(8,128)(2,1)} %all_to_all.32.grad_ref, bf16[256,4096]{1,0:T(8,128)(2,1)} %get-tuple-element.135.normed_ref, f32[256,128]{1,0:T(8,128)} %get-tuple-element.136.inv_ref), custom_call_target="tpu_custom_call" | custom-call | tf_op jit(solution)/shard_map/project_out/pallas_call | solution.py:478
  (37 shorter events, 3.0 us)
Async XLA Ops:
  86.1 3.7 %collective-permute-start.30 = (f32[8,384,128]{2,1,0:T(8,128)}, f32[8,384,128]{2,1,0:T(8,128)S(1)}, u32[]{:S(2)}, u32[]{:S(2)}) collective-permute-start(f32[8,384,128]{2,1,0:T(8,128)} %get-tuple-element.46), channel_id=1, source_target_pairs={{0,1},{1,0},{2,3},{3,2},{4,5},{5,4},{6,7},{7,6},{8,9},{9,8},{10,11... | collective-permute-start | bytes 4718600 | tf_op jit(solution)/shard_map/cond/branch_2_fun/ppermute | solution.py:495
  86.3 3.4 %collective-permute-start.31 = (f32[8,128]{1,0:T(8,128)}, f32[8,128]{1,0:T(8,128)S(1)}, u32[]{:S(2)}, u32[]{:S(2)}) collective-permute-start(f32[8,128]{1,0:T(8,128)} %get-tuple-element.47.top_ref), channel_id=1, source_target_pairs={{0,1},{1,0},{2,3},{3,2},{4,5},{5,4},{6,7},{7,6},{8,9},{9,8},{10,11... | collective-permute-start | bytes 12296 | tf_op jit(solution)/shard_map/cond/branch_2_fun/ppermute | solution.py:495
  89.8 0.6 copy-start.72
  89.8 1.2 copy-start.5
  95.2 5.1 %collective-permute-start.32 = (s16[25,16,128]{2,1,0:T(8,128)(2,1)}, s16[25,16,128]{2,1,0:T(8,128)(2,1)S(1)}, u32[]{:S(2)}, u32[]{:S(2)}) collective-permute-start(s16[25,16,128]{2,1,0:T(8,128)(2,1)} %get-tuple-element.49), channel_id=1, source_target_pairs={{0,2},{1,3},{2,0},{3,1},{4,6},{5,7},{6,4},{7,5},{8,10},{9,11},{10,... | collective-permute-start | bytes 307208 | tf_op jit(solution)/shard_map/cond/branch_2_fun/ppermute | solution.py:495
  95.5 6.3 %collective-permute-start.33 = (s16[25,16,128]{2,1,0:T(8,128)(2,1)}, s16[25,16,128]{2,1,0:T(8,128)(2,1)S(1)}, u32[]{:S(2)}, u32[]{:S(2)}) collective-permute-start(s16[25,16,128]{2,1,0:T(8,128)(2,1)} %get-tuple-element.50), channel_id=1, source_target_pairs={{0,4},{1,5},{2,6},{3,7},{4,0},{5,1},{6,2},{7,3},{8,12},{9,13},{10,... | collective-permute-start | bytes 307208 | tf_op jit(solution)/shard_map/cond/branch_2_fun/ppermute | solution.py:495
  96.0 8.4 %collective-permute-start.34 = (s16[25,16,128]{2,1,0:T(8,128)(2,1)}, s16[25,16,128]{2,1,0:T(8,128)(2,1)S(1)}, u32[]{:S(2)}, u32[]{:S(2)}) collective-permute-start(s16[25,16,128]{2,1,0:T(8,128)(2,1)} %get-tuple-element.51), channel_id=1, source_target_pairs={{0,6},{1,7},{2,4},{3,5},{4,2},{5,3},{6,0},{7,1},{8,14},{9,15},{10,... | collective-permute-start | bytes 307208 | tf_op jit(solution)/shard_map/cond/branch_2_fun/ppermute | solution.py:495
  97.8 6.5 %collective-permute-start.35 = (s16[25,16,128]{2,1,0:T(8,128)(2,1)}, s16[25,16,128]{2,1,0:T(8,128)(2,1)S(1)}, u32[]{:S(2)}, u32[]{:S(2)}) collective-permute-start(s16[25,16,128]{2,1,0:T(8,128)(2,1)} %get-tuple-element.52), channel_id=1, source_target_pairs={{0,8},{1,9},{2,10},{3,11},{4,12},{5,13},{6,14},{7,15},{8,0},{9,1},... | collective-permute-start | bytes 307208 | tf_op jit(solution)/shard_map/cond/branch_2_fun/ppermute | solution.py:495
  98.6 15.5 %collective-permute-start.36 = (s16[25,16,128]{2,1,0:T(8,128)(2,1)}, s16[25,16,128]{2,1,0:T(8,128)(2,1)S(1)}, u32[]{:S(2)}, u32[]{:S(2)}) collective-permute-start(s16[25,16,128]{2,1,0:T(8,128)(2,1)} %get-tuple-element.53), channel_id=1, source_target_pairs={{0,10},{1,11},{2,8},{3,9},{4,14},{5,15},{6,12},{7,13},{8,2},{9,3},... | collective-permute-start | bytes 307208 | tf_op jit(solution)/shard_map/cond/branch_2_fun/ppermute | solution.py:495
  100.3 13.9 %copy-start.49 = (s16[25,16,128]{2,1,0:T(8,128)(2,1)}, s16[25,16,128]{2,1,0:T(8,128)(2,1)S(1)}, u32[]{:S(2)}) copy-start(s16[25,16,128]{2,1,0:T(8,128)(2,1)S(1)} %collective-permute-done.32.refs_0_) | copy-start | bytes 307204 | tf_op jit(solution)/shard_map/cond
  100.3 13.9 %collective-permute-start.37 = (s16[25,16,128]{2,1,0:T(8,128)(2,1)}, s16[25,16,128]{2,1,0:T(8,128)(2,1)S(1)}, u32[]{:S(2)}, u32[]{:S(2)}) collective-permute-start(s16[25,16,128]{2,1,0:T(8,128)(2,1)} %get-tuple-element.54), channel_id=1, source_target_pairs={{0,12},{1,13},{2,14},{3,15},{4,8},{5,9},{6,10},{7,11},{8,4},{9,5},... | collective-permute-start | bytes 307208 | tf_op jit(solution)/shard_map/cond/branch_2_fun/ppermute | solution.py:495
  101.8 12.4 %copy-start.50 = (s16[25,16,128]{2,1,0:T(8,128)(2,1)}, s16[25,16,128]{2,1,0:T(8,128)(2,1)S(1)}, u32[]{:S(2)}) copy-start(s16[25,16,128]{2,1,0:T(8,128)(2,1)S(1)} %collective-permute-done.33.refs_1_) | copy-start | bytes 307204 | tf_op jit(solution)/shard_map/cond
  101.8 12.4 %collective-permute-start.38 = (s16[25,16,128]{2,1,0:T(8,128)(2,1)}, s16[25,16,128]{2,1,0:T(8,128)(2,1)S(1)}, u32[]{:S(2)}, u32[]{:S(2)}) collective-permute-start(s16[25,16,128]{2,1,0:T(8,128)(2,1)} %get-tuple-element.55), channel_id=1, source_target_pairs={{0,14},{1,15},{2,12},{3,13},{4,10},{5,11},{6,8},{7,9},{8,6},{9,7},... | collective-permute-start | bytes 307208 | tf_op jit(solution)/shard_map/cond/branch_2_fun/ppermute | solution.py:495
  104.4 9.9 %copy-start.51 = (s16[25,16,128]{2,1,0:T(8,128)(2,1)}, s16[25,16,128]{2,1,0:T(8,128)(2,1)S(1)}, u32[]{:S(2)}) copy-start(s16[25,16,128]{2,1,0:T(8,128)(2,1)S(1)} %collective-permute-done.34.refs_2_) | copy-start | bytes 307204 | tf_op jit(solution)/shard_map/cond
  104.4 9.9 %copy-start.52 = (s16[25,16,128]{2,1,0:T(8,128)(2,1)}, s16[25,16,128]{2,1,0:T(8,128)(2,1)S(1)}, u32[]{:S(2)}) copy-start(s16[25,16,128]{2,1,0:T(8,128)(2,1)S(1)} %collective-permute-done.35.refs_3_) | copy-start | bytes 307204 | tf_op jit(solution)/shard_map/cond
  114.2 0.6 copy-start.53
  114.2 0.7 copy-start.54
  114.2 0.7 copy-start.55
  118.1 7.4 %collective-permute-start.39 = (bf16[1,25,16,128]{3,2,1,0:T(8,128)(2,1)}, bf16[1,25,16,128]{3,2,1,0:T(8,128)(2,1)S(1)}, u32[]{:S(2)}, u32[]{:S(2)}) collective-permute-start(bf16[1,25,16,128]{3,2,1,0:T(8,128)(2,1)} %bitcast.41), channel_id=1, source_target_pairs={{0,8},{1,9},{2,10},{3,11},{4,12},{5,13},{6,14},{7,15},{8,0},{9,1},... | collective-permute-start | bytes 307208 | tf_op jit(solution)/shard_map/cond/branch_2_fun/ppermute | solution.py:495
  126.4 5.1 %collective-permute-start.40 = (bf16[2,25,16,128]{3,2,1,0:T(8,128)(2,1)S(1)}, bf16[2,25,16,128]{3,2,1,0:T(8,128)(2,1)S(1)}, u32[]{:S(2)}, u32[]{:S(2)}) collective-permute-start(bf16[2,25,16,128]{3,2,1,0:T(8,128)(2,1)S(1)} %pad_maximum_fusion.2), channel_id=1, source_target_pairs={{0,4},{1,5},{2,6},{3,7},{4,0},{5,1},{6,2},{7,3},{8,12},{9,13},{10,... | collective-permute-start | bytes 614408 | tf_op jit(solution)/shard_map/cond/branch_2_fun/ppermute | solution.py:495
  129.3 3.7 %collective-permute-start.41 = (bf16[1,25,16,128]{3,2,1,0:T(8,128)(2,1)}, bf16[1,25,16,128]{3,2,1,0:T(8,128)(2,1)S(1)}, u32[]{:S(2)}, u32[]{:S(2)}) collective-permute-start(bf16[1,25,16,128]{3,2,1,0:T(8,128)(2,1)} %bitcast.43), channel_id=1, source_target_pairs={{0,2},{1,3},{2,0},{3,1},{4,6},{5,7},{6,4},{7,5},{8,10},{9,11},{10,... | collective-permute-start | bytes 307208 | tf_op jit(solution)/shard_map/cond/branch_2_fun/ppermute | solution.py:495
  129.7 4.7 %collective-permute-start.42 = (bf16[1,25,16,128]{3,2,1,0:T(8,128)(2,1)S(1)}, bf16[1,25,16,128]{3,2,1,0:T(8,128)(2,1)S(1)}, u32[]{:S(2)}, u32[]{:S(2)}) collective-permute-start(bf16[1,25,16,128]{3,2,1,0:T(8,128)(2,1)S(1)} %collective-permute-done.39), channel_id=1, source_target_pairs={{0,2},{1,3},{2,0},{3,1},{4,6},{5,7},{6,4},{7,5},{8,10},{9,11},{10,... | collective-permute-start | bytes 307208 | tf_op jit(solution)/shard_map/cond/branch_2_fun/ppermute | solution.py:495
  131.6 6.0 %collective-permute-start.43 = (bf16[2,25,16,128]{3,2,1,0:T(8,128)(2,1)S(1)}, bf16[2,25,16,128]{3,2,1,0:T(8,128)(2,1)S(1)}, u32[]{:S(2)}, u32[]{:S(2)}) collective-permute-start(bf16[2,25,16,128]{3,2,1,0:T(8,128)(2,1)S(1)} %collective-permute-done.40), channel_id=1, source_target_pairs={{0,2},{1,3},{2,0},{3,1},{4,6},{5,7},{6,4},{7,5},{8,10},{9,11},{10,... | collective-permute-start | bytes 614408 | tf_op jit(solution)/shard_map/cond/branch_2_fun/ppermute | solution.py:495
  137.6 6.9 %copy-start.13 = (bf16[8,25,16,128]{3,2,1,0:T(8,128)(2,1)}, bf16[8,25,16,128]{3,2,1,0:T(8,128)(2,1)S(1)}, u32[]{:S(2)}) copy-start(bf16[8,25,16,128]{3,2,1,0:T(8,128)(2,1)S(1)} %constant_dynamic-update-slice_fusion.12.refs_0_) | copy-start | bytes 2457604 | tf_op jit(solution)/shard_map/cond
  137.6 6.9 %collective-permute-start.44 = (bf16[8,25,16,128]{3,2,1,0:T(8,128)(2,1)S(1)}, bf16[8,25,16,128]{3,2,1,0:T(8,128)(2,1)S(1)}, u32[]{:S(2)}, u32[]{:S(2)}) collective-permute-start(bf16[8,25,16,128]{3,2,1,0:T(8,128)(2,1)S(1)} %constant_dynamic-update-slice_fusion.12.refs_0_), channel_id=1, source_target_pairs={{0,1},{1,0},{2,3},{3,2},{4,5},{5,4},{6,7},{7,6},{8,9},{9,8},{10,11... | collective-permute-start | bytes 2457608 | tf_op jit(solution)/shard_map/cond/branch_2_fun/ppermute | solution.py:495
  144.5 0.9 copy-start.18
where the time goes:
time: 221 us
  blocking collectives  110 us (50%)
  Pallas kernels  56.5 us (26%)
  starting transfers between devices  23.6 us (11%)
  waiting for transfers between devices  23.5 us (11%)
  local copies, waits for them, and re-layouts  3.73 us (2%)
    all_to_all x1, blocking collectives, feature_plan(): lax.all_to_all(embedding, 'pb', split_axis=0, concat_axis=0, tiled=True)  59.2 us
    all_to_all x1, blocking collectives, feature_plan(): lax.all_to_all(grads, 'pb', split_axis=0, concat_axis=0, tiled=True)  51.2 us
    ppermute x15, starting transfers between devices, swapped(): return lax.ppermute(value, 'pb', pairs)  23.6 us
    ppermute x15, waiting for transfers between devices, swapped(): return lax.ppermute(value, 'pb', pairs)  23.5 us
    pallas_call x1, Pallas kernels, score_call(): pl.pallas_call(functools.partial(score_kernel, blocks, pairs, window), in...  19.1 us
    pallas_call x1, Pallas kernels, grad_call(): pl.pallas_call(functools.partial(grad_kernel, blocks, pairs, window), in_...  18.9 us
    pallas_call x1, Pallas kernels, norm_call(): pl.pallas_call(norm_kernel, in_specs=[whole, whole, whole, whole, pl.Bloc...  5.66 us
    pallas_call x1, Pallas kernels, project_call(): pl.pallas_call(project_kernel, grid=(seqs // rows,), in_specs=[pl.BlockSp...  5.38 us
  transfers between devices with their start and end apart: 15, of which 8 were waited for; matrix products, arithmetic and copies ran while one was open for 0% of the time, Pallas kernels for 0%

commit v1 on v0

--- a/solution.py
+++ b/solution.py
@@ -13,7 +13,7 @@
 lanes = 128
 bound_steps = 256.0
 code_steps = 32000.0
-vmem_limit = 56 * 1024 * 1024
+mebibyte = 1024 * 1024
 
 
 def spread(target, at, value):
@@ -95,7 +95,7 @@
             jax.ShapeDtypeStruct((seqs, lanes), jnp.float32),
             jax.ShapeDtypeStruct((parts, seqs + 16, piece), jnp.bfloat16),
         ],
-        compiler_params=pltpu.CompilerParams(vmem_limit_bytes=vmem_limit),
+        compiler_params=pltpu.CompilerParams(vmem_limit_bytes=14 * mebibyte),
         name="norm_rows",
     )(last_row, hidden, gain, owners, hard_negatives)
 
@@ -222,7 +222,7 @@
             pltpu.SMEM((blocks, lanes), jnp.int32),
             pltpu.SemaphoreType.DMA((2,)),
         ],
-        compiler_params=pltpu.CompilerParams(vmem_limit_bytes=vmem_limit),
+        compiler_params=pltpu.CompilerParams(vmem_limit_bytes=22 * mebibyte),
         name="partial_scores",
     )(embedded)
 
@@ -264,7 +264,7 @@
         in_specs=[whole] * 4,
         out_specs=[whole] * chips,
         out_shape=[jax.ShapeDtypeStruct((rows, pairs), jnp.float32)] + [coded] * (chips - 1),
-        compiler_params=pltpu.CompilerParams(vmem_limit_bytes=vmem_limit),
+        compiler_params=pltpu.CompilerParams(vmem_limit_bytes=12 * mebibyte),
         name="merge_scores",
     )(mine, other, top, other_top)
 
@@ -340,7 +340,7 @@
             pltpu.VMEM((room, fine, pairs), jnp.float32),
             pltpu.VMEM((blocks * fine, (window + 1) * pairs), jnp.float32),
         ],
-        compiler_params=pltpu.CompilerParams(vmem_limit_bytes=vmem_limit),
+        compiler_params=pltpu.CompilerParams(vmem_limit_bytes=8 * mebibyte),
         name="softmax_rows",
     )(place, own_scores, *codes)
 
@@ -452,7 +452,7 @@
             pltpu.VMEM((blocks, room, pairs // blocks, pairs), jnp.float32),
             pltpu.VMEM((2 * pairs, (window + 2) * pairs), jnp.bfloat16),
         ],
-        compiler_params=pltpu.CompilerParams(vmem_limit_bytes=vmem_limit),
+        compiler_params=pltpu.CompilerParams(vmem_limit_bytes=26 * mebibyte),
         name="slice_grads",
     )(own, place, queries, documents, *parts)
 
@@ -485,7 +485,7 @@
         ],
         out_specs=pl.BlockSpec((rows, width), lambda i: (i, 0)),
         out_shape=jax.ShapeDtypeStruct((seqs, width), jnp.float32),
-        compiler_params=pltpu.CompilerParams(vmem_limit_bytes=vmem_limit),
+        compiler_params=pltpu.CompilerParams(vmem_limit_bytes=10 * mebibyte),
         name="project_out",
     )(returned, normed, inverse)
 

time: 221 us -> 214 us (0.968)
  Pallas kernels: 56.5 us -> 46.3 us
  waiting for transfers between devices: 23.5 us -> 27.1 us
    unnamed x0 -> x12, local copies, waits for them, and re-layouts: none -> 5.65 us
    ppermute x15, waiting for transfers between devices: 23.5 us -> 27.1 us  [swapped(): return lax.ppermute(value, 'pb', pairs)]
    cond x27 -> x5, local copies, waits for them, and re-layouts: 3.7 us -> 0.08 us
    pallas_call x1, Pallas kernels: 5.66 us -> 2.91 us  [norm_call(): pl.pallas_call(norm_kernel, in_specs=[whole, whole, whole, whole, pl.Bloc...]
    pallas_call x1, Pallas kernels: 4.24 us -> 1.52 us  [merge_call(): pl.pallas_call(merge_kernel, in_specs=[whole] * 4, out_specs=[whole] * ch...]
where the time goes in v1:
time: 214 us
  blocking collectives  110 us (51%)
  Pallas kernels  46.3 us (22%)
  waiting for transfers between devices  27.1 us (13%)
  starting transfers between devices  22.8 us (11%)
  local copies, waits for them, and re-layouts  5.77 us (3%)
    all_to_all x1, blocking collectives, feature_plan(): lax.all_to_all(embedding, 'pb', split_axis=0, concat_axis=0, tiled=True)  59 us
    all_to_all x1, blocking collectives, feature_plan(): lax.all_to_all(grads, 'pb', split_axis=0, concat_axis=0, tiled=True)  51.1 us
    ppermute x15, waiting for transfers between devices, swapped(): return lax.ppermute(value, 'pb', pairs)  27.1 us
    ppermute x15, starting transfers between devices, swapped(): return lax.ppermute(value, 'pb', pairs)  22.8 us
    pallas_call x1, Pallas kernels, score_call(): pl.pallas_call(functools.partial(score_kernel, blocks, pairs, window), in...  18.9 us
    pallas_call x1, Pallas kernels, grad_call(): pl.pallas_call(functools.partial(grad_kernel, blocks, pairs, window), in_...  17.7 us
    unnamed x12, local copies, waits for them, and re-layouts  5.65 us
  transfers between devices with their start and end apart: 15, of which 8 were waited for; matrix products, arithmetic and copies ran while one was open for 0% of the time, Pallas kernels for 0%

profile of v1, /device:TPU:1, one launch (start us, length us, event | category | flops | bytes accessed | tf_op | source)
XLA Modules:
  0.0 214.4 jit_solution(12877214594355013897)
XLA Ops:
  0.6 1.6 copy-done
  2.2 0.7 copy-done.1
  2.9 0.7 copy-done.2
  3.6 0.7 copy-done.3
  4.3 0.7 copy-done.4
  4.9 2.9 %norm_rows.1 = (bf16[256,4096]{1,0:T(8,128)(2,1)S(1)}, f32[256,128]{1,0:T(8,128)S(1)}, bf16[16,272,256]{2,1,0:T(8,128)(2,1)S(1)}) custom-call(s32[1,256]{1,0:T(1,128)S(1)} %copy-done.2, bf16[256,4096]{1,0:T(8,128)(2,1)S(1)} %copy-done, bf16[4096]{0:T(1024)(128)(2,1)S(1)} %copy-done.1, s32[2,128]{1,0:T(2,128)S(1)} %bitcast.50, s32[1,4]{1,0:T(1,128)S(1)} %copy-done.4), custom_call_target="tpu_custom_call" | custom-call | tf_op jit(solution)/shard_map/norm_rows/pallas_call | solution.py:89
  7.9 59.0 %all_to_all.31 = bf16[16,272,256]{2,1,0:T(8,128)(2,1)S(1)} all-to-all(bf16[16,272,256]{2,1,0:T(8,128)(2,1)S(1)} %get-tuple-element.133), channel_id=1, replica_groups=mesh['groups'=2,'pb'=16] {'pb'}, dimensions={0} | all-to-all | bytes 4456448 | tf_op jit(solution)/shard_map/all_to_all | solution.py:543
  66.9 1.4 copy-done.5
  69.5 90.5 %conditional.1 = (bf16[16,256,256]{2,1,0:T(8,128)(2,1)S(1)}, f32[1]{0:T(128)}) conditional(s32[]{:T(128)} %clamp.3, bf16[16,272,256]{2,1,0:T(8,128)(2,1)} %copy-done.5, bf16[16,272,256]{2,1,0:T(8,128)(2,1)} %copy-done.5, bf16[16,272,256]{2,1,0:T(8,128)(2,1)} %copy-done.5, ...), branch_computations={%region_1.0_spmd, %region_2.0_spmd, %region_3.0_spmd, %region_4.0_... | conditional | flops 167936 | bytes 28639848 | solution.py:548
  69.8 18.9 %partial_scores.10 = (bf16[2048,256]{1,0:T(8,128)(2,1)S(1)}, bf16[2560,256]{1,0:T(8,128)(2,1)S(1)}, f32[8,416,128]{2,1,0:T(8,128)S(1)}, f32[8,416,128]{2,1,0:T(8...) custom-call(bf16[16,272,256]{2,1,0:T(8,128)(2,1)} %refs_0_.3), custom_call_target="tpu_custom_call" | custom-call | tf_op jit(solution)/shard_map/cond/branch_3_fun/partial_scores/pallas_call | solution.py:203
  89.3 3.1 %collective-permute-done.46.other_top_ref = f32[8,128]{1,0:T(8,128)S(1)} collective-permute-done((f32[8,128]{1,0:T(8,128)S(1)}, f32[8,128]{1,0:T(8,128)S(1)}, u32[]{:S(2)}, u32[]{:S(2)}) %collective-permute-start.46) | collective-permute-done | bytes 4128 | tf_op jit(solution)/shard_map/cond/branch_3_fun/ppermute | solution.py:495
  92.4 1.5 merge_scores.10
  94.8 1.8 collective-permute-start.49
  96.6 0.8 collective-permute-start.50
  97.4 1.6 collective-permute-start.51
  99.0 1.5 collective-permute-start.52
  100.6 2.6 %collective-permute-start.53 = (s16[27,16,128]{2,1,0:T(8,128)(2,1)S(1)}, s16[27,16,128]{2,1,0:T(8,128)(2,1)S(1)}, u32[]{:S(2)}, u32[]{:S(2)}) collective-permute-start(s16[27,16,128]{2,1,0:T(8,128)(2,1)S(1)} %get-tuple-element.72), channel_id=1, source_target_pairs={{0,14},{1,15},{2,12},{3,13},{4,10},{5,11},{6,8},{7,9},{8,6},{9,7},... | collective-permute-start | bytes 331784 | tf_op jit(solution)/shard_map/cond/branch_3_fun/ppermute | solution.py:495
  103.1 0.8 collective-permute-done.49.refs_2_
  103.9 9.9 %collective-permute-done.51.refs_4_ = s16[27,16,128]{2,1,0:T(8,128)(2,1)S(1)} collective-permute-done((s16[27,16,128]{2,1,0:T(8,128)(2,1)S(1)}, s16[27,16,128]{2,1,0:T(8,128)(2,1)S(1)}, u32[]{:S(2)}, u32[]{:S(2)}) %collective-permute-start.51) | collective-permute-done | bytes 110624 | tf_op jit(solution)/shard_map/cond/branch_3_fun/ppermute | solution.py:495
  113.8 1.9 softmax_rows.10
  115.7 5.6 %collective-permute-start.54 = (bf16[1,27,16,128]{3,2,1,0:T(8,128)(2,1)S(1)}, bf16[1,27,16,128]{3,2,1,0:T(8,128)(2,1)S(1)}, u32[]{:S(2)}, u32[]{:S(2)}) collective-permute-start(bf16[1,27,16,128]{3,2,1,0:T(8,128)(2,1)S(1)} %bitcast.38), channel_id=1, source_target_pairs={{0,8},{1,9},{2,10},{3,11},{4,12},{5,13},{6,14},{7,15},{8,0},{9,1},... | collective-permute-start | bytes 331784 | tf_op jit(solution)/shard_map/cond/branch_3_fun/ppermute | solution.py:495
  121.3 2.1 collective-permute-done.54
  123.5 2.0 collective-permute-start.55
  125.8 1.2 collective-permute-start.57
  127.0 2.0 collective-permute-done.55
  129.2 1.2 collective-permute-done.57
  130.4 5.9 %collective-permute-done.58 = bf16[2,27,16,128]{3,2,1,0:T(8,128)(2,1)S(1)} collective-permute-done((bf16[2,27,16,128]{3,2,1,0:T(8,128)(2,1)S(1)}, bf16[2,27,16,128]{3,2,1,0:T(8,128)(2,1)S(1)}, u32[]{:S(2)}, u32[]{:S(2)}) %collective-permute-start.58) | collective-permute-done | bytes 221216 | tf_op jit(solution)/shard_map/cond/branch_3_fun/ppermute | solution.py:495
  136.3 3.9 %collective-permute-start.59 = (bf16[8,27,16,128]{3,2,1,0:T(8,128)(2,1)S(1)}, bf16[8,27,16,128]{3,2,1,0:T(8,128)(2,1)S(1)}, u32[]{:S(2)}, u32[]{:S(2)}) collective-permute-start(bf16[8,27,16,128]{3,2,1,0:T(8,128)(2,1)S(1)} %constant_dynamic-update-slice_fusion.18.refs_0_), channel_id=1, source_target_pairs={{0,1},{1,0},{2,3},{3,2},{4,5},{5,4},{6,7},{7,6},{8,9},{9,8},{10,11... | collective-permute-start | bytes 2654216 | tf_op jit(solution)/shard_map/cond/branch_3_fun/ppermute | solution.py:495
  140.2 2.1 collective-permute-done.59.refs_1_
  142.3 17.7 %slice_grads.10 = (bf16[16,256,256]{2,1,0:T(8,128)(2,1)S(1)}, f32[1,128]{1,0:T(1,128)}) custom-call(s32[16,256]{1,0:T(8,128)S(1)} %get-tuple-element.58.own_ref, s32[5,16]{1,0:T(8,128)S(1)} %get-tuple-element.59.place_ref, bf16[2048,256]{1,0:T(8,128)(2,1)S(1)} %get-tuple-element.60.q_ref, bf16[2560,256]{1,0:T(8,128)(2,1)S(1)} %get-tuple-element.61.d_ref, ...), custom_call_target="tpu_custom_call" | custom-call | tf_op jit(solution)/shard_map/cond/branch_3_fun/slice_grads/pallas_call | solution.py:440
  160.0 51.1 %all_to_all.32.grad_ref = bf16[16,256,256]{2,1,0:T(8,128)(2,1)S(1)} all-to-all(bf16[16,256,256]{2,1,0:T(8,128)(2,1)S(1)} %get-tuple-element.134), channel_id=1, replica_groups=mesh['groups'=2,'pb'=16] {'pb'}, dimensions={0} | all-to-all | bytes 4194304 | tf_op jit(solution)/shard_map/all_to_all | solution.py:556
  211.1 3.3 %project_out.1 = f32[256,4096]{1,0:T(8,128)} custom-call(bf16[16,256,256]{2,1,0:T(8,128)(2,1)S(1)} %all_to_all.32.grad_ref, bf16[256,4096]{1,0:T(8,128)(2,1)S(1)} %get-tuple-element.135.normed_ref, f32[256,128]{1,0:T(8,128)S(1)} %get-tuple-element.136.inv_ref), custom_call_target="tpu_custom_call" | custom-call | tf_op jit(solution)/shard_map/project_out/pallas_call | solution.py:478
  (27 shorter events, 2.6 us)
Async XLA Ops:
  0.6 1.6 copy-start
  2.2 0.7 copy-start.1
  2.9 0.7 copy-start.2
  3.6 0.7 copy-start.3
  4.3 0.7 copy-start.4
  66.9 1.4 copy-start.5
  88.7 3.7 %collective-permute-start.45 = (f32[8,416,128]{2,1,0:T(8,128)S(1)}, f32[8,416,128]{2,1,0:T(8,128)S(1)}, u32[]{:S(2)}, u32[]{:S(2)}) collective-permute-start(f32[8,416,128]{2,1,0:T(8,128)S(1)} %get-tuple-element.63), channel_id=1, source_target_pairs={{0,1},{1,0},{2,3},{3,2},{4,5},{5,4},{6,7},{7,6},{8,9},{9,8},{10,11... | collective-permute-start | bytes 5111816 | tf_op jit(solution)/shard_map/cond/branch_3_fun/ppermute | solution.py:495
  88.9 3.4 %collective-permute-start.46 = (f32[8,128]{1,0:T(8,128)S(1)}, f32[8,128]{1,0:T(8,128)S(1)}, u32[]{:S(2)}, u32[]{:S(2)}) collective-permute-start(f32[8,128]{1,0:T(8,128)S(1)} %get-tuple-element.64.top_ref), channel_id=1, source_target_pairs={{0,1},{1,0},{2,3},{3,2},{4,5},{5,4},{6,7},{7,6},{8,9},{9,8},{10,11... | collective-permute-start | bytes 12296 | tf_op jit(solution)/shard_map/cond/branch_3_fun/ppermute | solution.py:495
  93.9 5.2 %collective-permute-start.47 = (s16[27,16,128]{2,1,0:T(8,128)(2,1)S(1)}, s16[27,16,128]{2,1,0:T(8,128)(2,1)S(1)}, u32[]{:S(2)}, u32[]{:S(2)}) collective-permute-start(s16[27,16,128]{2,1,0:T(8,128)(2,1)S(1)} %get-tuple-element.66), channel_id=1, source_target_pairs={{0,2},{1,3},{2,0},{3,1},{4,6},{5,7},{6,4},{7,5},{8,10},{9,11},{10,... | collective-permute-start | bytes 331784 | tf_op jit(solution)/shard_map/cond/branch_3_fun/ppermute | solution.py:495
  94.3 6.3 %collective-permute-start.48 = (s16[27,16,128]{2,1,0:T(8,128)(2,1)S(1)}, s16[27,16,128]{2,1,0:T(8,128)(2,1)S(1)}, u32[]{:S(2)}, u32[]{:S(2)}) collective-permute-start(s16[27,16,128]{2,1,0:T(8,128)(2,1)S(1)} %get-tuple-element.67), channel_id=1, source_target_pairs={{0,4},{1,5},{2,6},{3,7},{4,0},{5,1},{6,2},{7,3},{8,12},{9,13},{10,... | collective-permute-start | bytes 331784 | tf_op jit(solution)/shard_map/cond/branch_3_fun/ppermute | solution.py:495
  94.8 9.1 %collective-permute-start.49 = (s16[27,16,128]{2,1,0:T(8,128)(2,1)S(1)}, s16[27,16,128]{2,1,0:T(8,128)(2,1)S(1)}, u32[]{:S(2)}, u32[]{:S(2)}) collective-permute-start(s16[27,16,128]{2,1,0:T(8,128)(2,1)S(1)} %get-tuple-element.68), channel_id=1, source_target_pairs={{0,6},{1,7},{2,4},{3,5},{4,2},{5,3},{6,0},{7,1},{8,14},{9,15},{10,... | collective-permute-start | bytes 331784 | tf_op jit(solution)/shard_map/cond/branch_3_fun/ppermute | solution.py:495
  96.6 7.3 %collective-permute-start.50 = (s16[27,16,128]{2,1,0:T(8,128)(2,1)S(1)}, s16[27,16,128]{2,1,0:T(8,128)(2,1)S(1)}, u32[]{:S(2)}, u32[]{:S(2)}) collective-permute-start(s16[27,16,128]{2,1,0:T(8,128)(2,1)S(1)} %get-tuple-element.69), channel_id=1, source_target_pairs={{0,8},{1,9},{2,10},{3,11},{4,12},{5,13},{6,14},{7,15},{8,0},{9,1},... | collective-permute-start | bytes 331784 | tf_op jit(solution)/shard_map/cond/branch_3_fun/ppermute | solution.py:495
  97.4 16.4 %collective-permute-start.51 = (s16[27,16,128]{2,1,0:T(8,128)(2,1)S(1)}, s16[27,16,128]{2,1,0:T(8,128)(2,1)S(1)}, u32[]{:S(2)}, u32[]{:S(2)}) collective-permute-start(s16[27,16,128]{2,1,0:T(8,128)(2,1)S(1)} %get-tuple-element.70), channel_id=1, source_target_pairs={{0,10},{1,11},{2,8},{3,9},{4,14},{5,15},{6,12},{7,13},{8,2},{9,3},... | collective-permute-start | bytes 331784 | tf_op jit(solution)/shard_map/cond/branch_3_fun/ppermute | solution.py:495
  99.0 14.7 %collective-permute-start.52 = (s16[27,16,128]{2,1,0:T(8,128)(2,1)S(1)}, s16[27,16,128]{2,1,0:T(8,128)(2,1)S(1)}, u32[]{:S(2)}, u32[]{:S(2)}) collective-permute-start(s16[27,16,128]{2,1,0:T(8,128)(2,1)S(1)} %get-tuple-element.71), channel_id=1, source_target_pairs={{0,12},{1,13},{2,14},{3,15},{4,8},{5,9},{6,10},{7,11},{8,4},{9,5},... | collective-permute-start | bytes 331784 | tf_op jit(solution)/shard_map/cond/branch_3_fun/ppermute | solution.py:495
  100.6 13.2 %collective-permute-start.53 = (s16[27,16,128]{2,1,0:T(8,128)(2,1)S(1)}, s16[27,16,128]{2,1,0:T(8,128)(2,1)S(1)}, u32[]{:S(2)}, u32[]{:S(2)}) collective-permute-start(s16[27,16,128]{2,1,0:T(8,128)(2,1)S(1)} %get-tuple-element.72), channel_id=1, source_target_pairs={{0,14},{1,15},{2,12},{3,13},{4,10},{5,11},{6,8},{7,9},{8,6},{9,7},... | collective-permute-start | bytes 331784 | tf_op jit(solution)/shard_map/cond/branch_3_fun/ppermute | solution.py:495
  115.7 7.7 %collective-permute-start.54 = (bf16[1,27,16,128]{3,2,1,0:T(8,128)(2,1)S(1)}, bf16[1,27,16,128]{3,2,1,0:T(8,128)(2,1)S(1)}, u32[]{:S(2)}, u32[]{:S(2)}) collective-permute-start(bf16[1,27,16,128]{3,2,1,0:T(8,128)(2,1)S(1)} %bitcast.38), channel_id=1, source_target_pairs={{0,8},{1,9},{2,10},{3,11},{4,12},{5,13},{6,14},{7,15},{8,0},{9,1},... | collective-permute-start | bytes 331784 | tf_op jit(solution)/shard_map/cond/branch_3_fun/ppermute | solution.py:495
  123.5 5.6 %collective-permute-start.55 = (bf16[2,27,16,128]{3,2,1,0:T(8,128)(2,1)S(1)}, bf16[2,27,16,128]{3,2,1,0:T(8,128)(2,1)S(1)}, u32[]{:S(2)}, u32[]{:S(2)}) collective-permute-start(bf16[2,27,16,128]{3,2,1,0:T(8,128)(2,1)S(1)} %pad_maximum_fusion.3), channel_id=1, source_target_pairs={{0,4},{1,5},{2,6},{3,7},{4,0},{5,1},{6,2},{7,3},{8,12},{9,13},{10,... | collective-permute-start | bytes 663560 | tf_op jit(solution)/shard_map/cond/branch_3_fun/ppermute | solution.py:495
  125.5 3.7 %collective-permute-start.56 = (bf16[1,27,16,128]{3,2,1,0:T(8,128)(2,1)S(1)}, bf16[1,27,16,128]{3,2,1,0:T(8,128)(2,1)S(1)}, u32[]{:S(2)}, u32[]{:S(2)}) collective-permute-start(bf16[1,27,16,128]{3,2,1,0:T(8,128)(2,1)S(1)} %bitcast.40), channel_id=1, source_target_pairs={{0,2},{1,3},{2,0},{3,1},{4,6},{5,7},{6,4},{7,5},{8,10},{9,11},{10,... | collective-permute-start | bytes 331784 | tf_op jit(solution)/shard_map/cond/branch_3_fun/ppermute | solution.py:495
  125.8 4.6 %collective-permute-start.57 = (bf16[1,27,16,128]{3,2,1,0:T(8,128)(2,1)S(1)}, bf16[1,27,16,128]{3,2,1,0:T(8,128)(2,1)S(1)}, u32[]{:S(2)}, u32[]{:S(2)}) collective-permute-start(bf16[1,27,16,128]{3,2,1,0:T(8,128)(2,1)S(1)} %collective-permute-done.54), channel_id=1, source_target_pairs={{0,2},{1,3},{2,0},{3,1},{4,6},{5,7},{6,4},{7,5},{8,10},{9,11},{10,... | collective-permute-start | bytes 331784 | tf_op jit(solution)/shard_map/cond/branch_3_fun/ppermute | solution.py:495
  129.1 7.2 %collective-permute-start.58 = (bf16[2,27,16,128]{3,2,1,0:T(8,128)(2,1)S(1)}, bf16[2,27,16,128]{3,2,1,0:T(8,128)(2,1)S(1)}, u32[]{:S(2)}, u32[]{:S(2)}) collective-permute-start(bf16[2,27,16,128]{3,2,1,0:T(8,128)(2,1)S(1)} %collective-permute-done.55), channel_id=1, source_target_pairs={{0,2},{1,3},{2,0},{3,1},{4,6},{5,7},{6,4},{7,5},{8,10},{9,11},{10,... | collective-permute-start | bytes 663560 | tf_op jit(solution)/shard_map/cond/branch_3_fun/ppermute | solution.py:495
  136.3 5.9 %collective-permute-start.59 = (bf16[8,27,16,128]{3,2,1,0:T(8,128)(2,1)S(1)}, bf16[8,27,16,128]{3,2,1,0:T(8,128)(2,1)S(1)}, u32[]{:S(2)}, u32[]{:S(2)}) collective-permute-start(bf16[8,27,16,128]{3,2,1,0:T(8,128)(2,1)S(1)} %constant_dynamic-update-slice_fusion.18.refs_0_), channel_id=1, source_target_pairs={{0,1},{1,0},{2,3},{3,2},{4,5},{5,4},{6,7},{7,6},{8,9},{9,8},{10,11... | collective-permute-start | bytes 2654216 | tf_op jit(solution)/shard_map/cond/branch_3_fun/ppermute | solution.py:495

commit v2 on v1

--- a/solution.py
+++ b/solution.py
@@ -95,7 +95,7 @@
             jax.ShapeDtypeStruct((seqs, lanes), jnp.float32),
             jax.ShapeDtypeStruct((parts, seqs + 16, piece), jnp.bfloat16),
         ],
-        compiler_params=pltpu.CompilerParams(vmem_limit_bytes=14 * mebibyte),
+        compiler_params=pltpu.CompilerParams(vmem_limit_bytes=56 * mebibyte),
         name="norm_rows",
     )(last_row, hidden, gain, owners, hard_negatives)
 
@@ -106,8 +106,8 @@
     window,
     *refs,
 ):
-    emb_ref, q_ref, d_ref, mine_ref, other_ref, top_ref, own_ref, place_ref = refs[:-7]
-    wide, picked, tiles, facts, own, named, sems = refs[-7:]
+    emb_ref, q_ref, d_ref, mine_ref, other_ref, top_ref, own_ref, place_ref = refs[:-6]
+    wide, picked, facts, own, named, sems = refs[-6:]
     seqs = emb_ref.shape[1] - 16
     sent = emb_ref[:, seqs:, :].astype(jnp.float32)
     own_ref[...] = (sent[:, 0, :] + 256.0 * sent[:, 1, :]).astype(jnp.int32)
@@ -143,17 +143,13 @@
         return carry
 
     lax.fori_loop(used, mine_ref.shape[1] // fine, clear, 0)
-    unroll = 32
+    group = 32
 
     def pick_block(block, carry):
-        def pick_rows(step, inner):
-            base = pl.multiple_of(step * unroll, unroll)
-            rows = [wide[row_pair(own[block, base + k]), :] for k in range(unroll)]
-            for k in range(unroll):
-                picked[row_pair(base + k), :] = rows[k]
-            return inner
-
-        lax.fori_loop(0, 2 * pairs // unroll, pick_rows, 0)
+        for base in range(0, 2 * pairs, group):
+            rows = [wide[row_pair(own[block, base + k]), :] for k in range(group)]
+            for k in range(group):
+                picked[2 * (base + k) : 2 * (base + k + 1), :] = rows[k]
         at = pl.multiple_of(block * pairs, pairs)
         q_ref[pl.ds(at, pairs), :] = gathered(picked, 0, pairs).astype(jnp.bfloat16)
         d_ref[pl.ds(at, pairs), :] = gathered(picked, pairs, pairs).astype(jnp.bfloat16)
@@ -162,37 +158,36 @@
     lax.fori_loop(0, blocks, pick_block, 0)
     d_ref[blocks * pairs :, :] = d_ref[: window * pairs, :]
     even = lax.axis_index("pb") % 2 == 0
-    top_ref[...] = jnp.zeros_like(top_ref)
+    spare = mine_ref.shape[1] // fine - 1
 
     def score_blocks(step, carry):
         at = pl.multiple_of(step * 2 * pairs, 2 * pairs)
-        tiles[...] = inverse_temp * lax.dot_general(
+        tiles = inverse_temp * lax.dot_general(
             q_ref[pl.ds(at, 2 * pairs), :],
             d_ref[pl.ds(at, (window + 2) * pairs), :],
             (((1,), (1,)), ((), ())),
             preferred_element_type=jnp.float32,
         )
+        top = carry
         for half in range(2):
             for column in range(window + 1):
                 spot = place_ref[column, 2 * step + half]
-
-                @pl.when(spot >= 0)
-                def _():
-                    row = pl.multiple_of(spot * fine, fine)
-                    tile = tiles[
-                        half * pairs : (half + 1) * pairs,
-                        (half + column) * pairs : (half + column + 1) * pairs,
-                    ]
-                    parted = tile.reshape(blocks // 2, 2, fine, pairs)
-                    first, second = parted[:, 0], parted[:, 1]
-                    mine_ref[:, pl.ds(row, fine), :] = jnp.where(even, first, second)
-                    other_ref[:, pl.ds(row, fine), :] = jnp.where(even, second, first)
-                    size = jnp.maximum(jnp.abs(first), jnp.abs(second))
-                    top_ref[...] = jnp.maximum(top_ref[...], jnp.max(size, axis=0))
-
-        return carry
-
-    lax.fori_loop(0, blocks // 2, score_blocks, 0)
+                row = pl.multiple_of(jnp.where(spot >= 0, spot, spare) * fine, fine)
+                tile = tiles[
+                    half * pairs : (half + 1) * pairs,
+                    (half + column) * pairs : (half + column + 1) * pairs,
+                ]
+                parted = tile.reshape(blocks // 2, 2, fine, pairs)
+                first, second = parted[:, 0], parted[:, 1]
+                mine_ref[:, pl.ds(row, fine), :] = jnp.where(even, first, second)
+                other_ref[:, pl.ds(row, fine), :] = jnp.where(even, second, first)
+                size = jnp.maximum(jnp.abs(first), jnp.abs(second))
+                top = jnp.maximum(top, jnp.max(size, axis=0))
+        return top
+
+    top_ref[...] = lax.fori_loop(
+        0, blocks // 2, score_blocks, jnp.zeros((fine, pairs), jnp.float32)
+    )
 
 
 def score_call(embedded, room, blocks, pairs, window):
@@ -207,8 +202,8 @@
         out_shape=[
             jax.ShapeDtypeStruct((blocks * pairs, piece), jnp.bfloat16),
             jax.ShapeDtypeStruct(((blocks + window) * pairs, piece), jnp.bfloat16),
-            jax.ShapeDtypeStruct((blocks // 2, room * fine, pairs), jnp.float32),
-            jax.ShapeDtypeStruct((blocks // 2, room * fine, pairs), jnp.float32),
+            jax.ShapeDtypeStruct((blocks // 2, (room + 1) * fine, pairs), jnp.float32),
+            jax.ShapeDtypeStruct((blocks // 2, (room + 1) * fine, pairs), jnp.float32),
             jax.ShapeDtypeStruct((fine, pairs), jnp.float32),
             jax.ShapeDtypeStruct((blocks, 2 * pairs), jnp.int32),
             jax.ShapeDtypeStruct((window + 1, blocks), jnp.int32),
@@ -216,7 +211,6 @@
         scratch_shapes=[
             pltpu.VMEM((2 * blocks * (rows - 16), lanes), jnp.float32),
             pltpu.VMEM((4 * pairs, lanes), jnp.float32),
-            pltpu.VMEM((2 * pairs, (window + 2) * pairs), jnp.float32),
             pltpu.VMEM((blocks, lanes), jnp.int32),
             pltpu.SMEM((blocks, 2 * pairs), jnp.int32),
             pltpu.SMEM((blocks, lanes), jnp.int32),
@@ -228,7 +222,7 @@
 
 
 def merge_kernel(mine_ref, other_ref, top_ref, other_top_ref, own_ref, *code_refs):
-    chips, rows, pairs = mine_ref.shape
+    rows, pairs = own_ref.shape
     steps = code_refs[0].shape[0] - 1
     fine = rows // steps // 2
     chip = lax.axis_index("pb") // 2
@@ -239,7 +233,7 @@
     top = highest(top_ref) + highest(other_top_ref)
     bound = jnp.ceil(top * bound_steps) + 1.0
     scale = code_steps * bound_steps / bound
-    own_ref[...] = mine_ref[chip] + other_ref[chip]
+    own_ref[...] = mine_ref[chip, :rows] + other_ref[chip, :rows]
     for hop, code_ref in enumerate(code_refs):
         target = chip ^ (hop + 1)
 
@@ -257,6 +251,7 @@
 def merge_call(mine, other, top, other_top, blocks):
     chips, rows, pairs = mine.shape
     fine = pairs // blocks
+    rows = rows - fine
     whole = pl.BlockSpec(memory_space=pltpu.VMEM)
     coded = jax.ShapeDtypeStruct((rows // (2 * fine) + 1, 2 * fine, pairs), jnp.int16)
     return pl.pallas_call(
@@ -361,7 +356,7 @@
     room = packed.shape[1]
     me = lax.axis_index("pb")
     masks = swap_masks(blocks)
-    unroll = 32
+    group = 32
     losses = 0.0
     for part in part_refs:
         sent = part[:, room // 2].astype(jnp.float32)
@@ -383,14 +378,12 @@
     lax.fori_loop(0, room // 2, unpack, 0)
 
     def scatter_rows(block, offset, start):
-        def step_rows(step, inner):
-            base = pl.multiple_of(step * unroll, unroll)
-            rows = [picked[row_pair(start + base + k), :] for k in range(unroll)]
-            for k in range(unroll):
+        for base in range(0, pairs, group):
+            rows = [
+                picked[2 * (start + base + k) : 2 * (start + base + k + 1), :] for k in range(group)
+            ]
+            for k in range(group):
                 wide[row_pair(own_ref[block, offset + base + k]), :] = rows[k]
-            return inner
-
-        lax.fori_loop(0, pairs // unroll, step_rows, 0)
 
     def two_blocks(step, carry):
         for half in range(2):

time: 214 us -> 194 us (0.907)
  Pallas kernels: 46.3 us -> 32.4 us
  local copies, waits for them, and re-layouts: 5.77 us -> 0.11 us
    pallas_call x1, Pallas kernels: 18.9 us -> 10.1 us  [score_call(): pl.pallas_call(functools.partial(score_kernel, blocks, pairs, window), in...]
    pallas_call x1, Pallas kernels: 17.7 us -> 10.1 us  [grad_call(): pl.pallas_call(functools.partial(grad_kernel, blocks, pairs, window), in_...]
    unnamed x12 -> x4, local copies, waits for them, and re-layouts: 5.65 us -> 0.01 us
    pallas_call x1, Pallas kernels: 2.91 us -> 5.66 us  [norm_call(): pl.pallas_call(norm_kernel, in_specs=[whole, whole, whole, whole, pl.Bloc...]
  transfers between devices with their start and end apart: 15 -> 15, of which waited for: 8 -> 7; matrix products, arithmetic and copies ran while one was open for 0% -> 0% of each run, Pallas kernels for 0% -> 0%
where the time goes in v2:
time: 194 us; the launch traced here: 193 us
  blocking collectives  110 us (57%)
  Pallas kernels  32.4 us (17%)
  waiting for transfers between devices  25 us (13%)
  starting transfers between devices  22.7 us (12%)
    all_to_all x1, blocking collectives, feature_plan(): lax.all_to_all(embedding, 'pb', split_axis=0, concat_axis=0, tiled=True)  59.2 us
    all_to_all x1, blocking collectives, feature_plan(): lax.all_to_all(grads, 'pb', split_axis=0, concat_axis=0, tiled=True)  51.2 us
    ppermute x15, waiting for transfers between devices, swapped(): return lax.ppermute(value, 'pb', pairs)  25 us
    ppermute x15, starting transfers between devices, swapped(): return lax.ppermute(value, 'pb', pairs)  22.7 us
    pallas_call x1, Pallas kernels, score_call(): pl.pallas_call(functools.partial(score_kernel, blocks, pairs, window), in...  10.1 us
    pallas_call x1, Pallas kernels, grad_call(): pl.pallas_call(functools.partial(grad_kernel, blocks, pairs, window), in_...  10.1 us
    pallas_call x1, Pallas kernels, norm_call(): pl.pallas_call(norm_kernel, in_specs=[whole, whole, whole, whole, pl.Bloc...  5.66 us
  transfers between devices with their start and end apart: 15, of which 7 were waited for; matrix products, arithmetic and copies ran while one was open for 0% of the time, Pallas kernels for 0%

profile of v2, /device:TPU:1, one launch (start us, length us, event | category | flops | bytes accessed | tf_op | source)
XLA Modules:
  0.0 193.2 jit_solution(9163037317633534879)
XLA Ops:
  0.6 5.7 %norm_rows.1 = (bf16[256,4096]{1,0:T(8,128)(2,1)}, f32[256,128]{1,0:T(8,128)}, bf16[16,272,256]{2,1,0:T(8,128)(2,1)}) custom-call(s32[1,256]{1,0:T(1,128)} %last_ref.1, bf16[256,4096]{1,0:T(8,128)(2,1)} %hidden_ref.1, bf16[4096]{0:T(1024)(128)(2,1)} %gain_ref.1, s32[2,128]{1,0:T(2,128)} %bitcast.50, s32[1,4]{1,0:T(1,128)} %negative_ref.1), custom_call_target="tpu_custom_call" | custom-call | tf_op jit(solution)/shard_map/norm_rows/pallas_call | solution.py:89
  6.3 59.2 %all_to_all.31 = bf16[16,272,256]{2,1,0:T(8,128)(2,1)S(1)} all-to-all(bf16[16,272,256]{2,1,0:T(8,128)(2,1)} %get-tuple-element.133), channel_id=1, replica_groups=mesh['groups'=2,'pb'=16] {'pb'}, dimensions={0} | all-to-all | bytes 4456448 | tf_op jit(solution)/shard_map/all_to_all | solution.py:536
  65.5 0.6 fusion
  66.8 71.9 %conditional.1 = (bf16[16,256,256]{2,1,0:T(8,128)(2,1)S(1)}, f32[1]{0:T(128)}) conditional(s32[]{:T(128)} %clamp.3, bf16[16,272,256]{2,1,0:T(8,128)(2,1)S(1)} %all_to_all.31, bf16[16,272,256]{2,1,0:T(8,128)(2,1)S(1)} %all_to_all.31, bf16[16,272,256]{2,1,0:T(8,128)(2,1)S(1)} %all_to_all.31, ...), branch_computations={%region_1.0_spmd, %region_2.0_spmd, %region_3.0_spmd, %region_4.0_... | conditional | flops 167936 | bytes 28770920 | solution.py:541
  67.0 10.1 %partial_scores.9 = (bf16[2048,256]{1,0:T(8,128)(2,1)S(1)}, bf16[2560,256]{1,0:T(8,128)(2,1)S(1)}, f32[8,392,128]{2,1,0:T(8,128)S(1)}, f32[8,392,128]{2,1,0:T(8,...) custom-call(bf16[16,272,256]{2,1,0:T(8,128)(2,1)S(1)} %refs_0_.2), custom_call_target="tpu_custom_call" | custom-call | tf_op jit(solution)/shard_map/cond/branch_2_fun/partial_scores/pallas_call | solution.py:198
  77.1 0.3 collective-permute-start.30
  77.3 0.3 collective-permute-start.31
  77.7 3.0 %collective-permute-done.31.other_top_ref = f32[8,128]{1,0:T(8,128)S(1)} collective-permute-done((f32[8,128]{1,0:T(8,128)S(1)}, f32[8,128]{1,0:T(8,128)S(1)}, u32[]{:S(2)}, u32[]{:S(2)}) %collective-permute-start.31) | collective-permute-done | bytes 4128 | tf_op jit(solution)/shard_map/cond/branch_2_fun/ppermute | solution.py:488
  80.6 1.4 merge_scores.9
  82.0 0.4 collective-permute-start.32
  82.5 0.5 collective-permute-start.33
  82.9 1.8 collective-permute-start.34
  84.7 0.8 collective-permute-start.35
  85.6 1.6 collective-permute-start.36
  87.2 1.5 collective-permute-start.37
  88.7 2.6 %collective-permute-start.38 = (s16[25,16,128]{2,1,0:T(8,128)(2,1)S(1)}, s16[25,16,128]{2,1,0:T(8,128)(2,1)S(1)}, u32[]{:S(2)}, u32[]{:S(2)}) collective-permute-start(s16[25,16,128]{2,1,0:T(8,128)(2,1)S(1)} %get-tuple-element.55), channel_id=1, source_target_pairs={{0,14},{1,15},{2,12},{3,13},{4,10},{5,11},{6,8},{7,9},{8,6},{9,7},... | collective-permute-start | bytes 307208 | tf_op jit(solution)/shard_map/cond/branch_2_fun/ppermute | solution.py:488
  91.3 9.6 %collective-permute-done.36.refs_4_ = s16[25,16,128]{2,1,0:T(8,128)(2,1)S(1)} collective-permute-done((s16[25,16,128]{2,1,0:T(8,128)(2,1)S(1)}, s16[25,16,128]{2,1,0:T(8,128)(2,1)S(1)}, u32[]{:S(2)}, u32[]{:S(2)}) %collective-permute-start.36) | collective-permute-done | bytes 102432 | tf_op jit(solution)/shard_map/cond/branch_2_fun/ppermute | solution.py:488
  100.9 1.9 softmax_rows.9
  102.8 5.3 %collective-permute-start.39 = (bf16[1,25,16,128]{3,2,1,0:T(8,128)(2,1)S(1)}, bf16[1,25,16,128]{3,2,1,0:T(8,128)(2,1)S(1)}, u32[]{:S(2)}, u32[]{:S(2)}) collective-permute-start(bf16[1,25,16,128]{3,2,1,0:T(8,128)(2,1)S(1)} %bitcast.41), channel_id=1, source_target_pairs={{0,8},{1,9},{2,10},{3,11},{4,12},{5,13},{6,14},{7,15},{8,0},{9,1},... | collective-permute-start | bytes 307208 | tf_op jit(solution)/shard_map/cond/branch_2_fun/ppermute | solution.py:488
  108.1 2.1 %collective-permute-done.39 = bf16[1,25,16,128]{3,2,1,0:T(8,128)(2,1)S(1)} collective-permute-done((bf16[1,25,16,128]{3,2,1,0:T(8,128)(2,1)S(1)}, bf16[1,25,16,128]{3,2,1,0:T(8,128)(2,1)S(1)}, u32[]{:S(2)}, u32[]{:S(2)}) %collective-permute-start.39) | collective-permute-done | bytes 102432 | tf_op jit(solution)/shard_map/cond/branch_2_fun/ppermute | solution.py:488
  110.2 2.0 %collective-permute-start.40 = (bf16[2,25,16,128]{3,2,1,0:T(8,128)(2,1)S(1)}, bf16[2,25,16,128]{3,2,1,0:T(8,128)(2,1)S(1)}, u32[]{:S(2)}, u32[]{:S(2)}) collective-permute-start(bf16[2,25,16,128]{3,2,1,0:T(8,128)(2,1)S(1)} %pad_maximum_fusion.2), channel_id=1, source_target_pairs={{0,4},{1,5},{2,6},{3,7},{4,0},{5,1},{6,2},{7,3},{8,12},{9,13},{10,... | collective-permute-start | bytes 614408 | tf_op jit(solution)/shard_map/cond/branch_2_fun/ppermute | solution.py:488
  112.1 0.4 collective-permute-start.41
  112.6 1.1 collective-permute-start.42
  113.7 1.8 collective-permute-done.40
  115.4 0.2 collective-permute-start.43
  115.7 1.1 collective-permute-done.42
  116.8 5.6 %collective-permute-done.43 = bf16[2,25,16,128]{3,2,1,0:T(8,128)(2,1)S(1)} collective-permute-done((bf16[2,25,16,128]{3,2,1,0:T(8,128)(2,1)S(1)}, bf16[2,25,16,128]{3,2,1,0:T(8,128)(2,1)S(1)}, u32[]{:S(2)}, u32[]{:S(2)}) %collective-permute-start.43) | collective-permute-done | bytes 204832 | tf_op jit(solution)/shard_map/cond/branch_2_fun/ppermute | solution.py:488
  122.5 3.9 %collective-permute-start.44 = (bf16[8,25,16,128]{3,2,1,0:T(8,128)(2,1)S(1)}, bf16[8,25,16,128]{3,2,1,0:T(8,128)(2,1)S(1)}, u32[]{:S(2)}, u32[]{:S(2)}) collective-permute-start(bf16[8,25,16,128]{3,2,1,0:T(8,128)(2,1)S(1)} %constant_dynamic-update-slice_fusion.12.refs_0_), channel_id=1, source_target_pairs={{0,1},{1,0},{2,3},{3,2},{4,5},{5,4},{6,7},{7,6},{8,9},{9,8},{10,11... | collective-permute-start | bytes 2457608 | tf_op jit(solution)/shard_map/cond/branch_2_fun/ppermute | solution.py:488
  126.4 2.0 %collective-permute-done.44.refs_1_ = bf16[8,25,16,128]{3,2,1,0:T(8,128)(2,1)S(1)} collective-permute-done((bf16[8,25,16,128]{3,2,1,0:T(8,128)(2,1)S(1)}, bf16[8,25,16,128]{3,2,1,0:T(8,128)(2,1)S(1)}, u32[]{:S(2)}, u32[]{:S(2)}) %collective-permute-start.44) | collective-permute-done | bytes 819232 | tf_op jit(solution)/shard_map/cond/branch_2_fun/ppermute | solution.py:488
  128.3 10.1 %slice_grads.9 = (bf16[16,256,256]{2,1,0:T(8,128)(2,1)S(1)}, f32[1,128]{1,0:T(1,128)}) custom-call(s32[16,256]{1,0:T(8,128)S(1)} %get-tuple-element.41.own_ref, s32[5,16]{1,0:T(8,128)S(1)} %get-tuple-element.42.place_ref, bf16[2048,256]{1,0:T(8,128)(2,1)S(1)} %get-tuple-element.43.q_ref, bf16[2560,256]{1,0:T(8,128)(2,1)S(1)} %get-tuple-element.44.d_ref, ...), custom_call_target="tpu_custom_call" | custom-call | tf_op jit(solution)/shard_map/cond/branch_2_fun/slice_grads/pallas_call | solution.py:433
  138.7 51.2 %all_to_all.32.grad_ref = bf16[16,256,256]{2,1,0:T(8,128)(2,1)S(1)} all-to-all(bf16[16,256,256]{2,1,0:T(8,128)(2,1)S(1)} %get-tuple-element.134), channel_id=1, replica_groups=mesh['groups'=2,'pb'=16] {'pb'}, dimensions={0} | all-to-all | bytes 4194304 | tf_op jit(solution)/shard_map/all_to_all | solution.py:549
  189.9 3.3 %project_out.1 = f32[256,4096]{1,0:T(8,128)} custom-call(bf16[16,256,256]{2,1,0:T(8,128)(2,1)S(1)} %all_to_all.32.grad_ref, bf16[256,4096]{1,0:T(8,128)(2,1)S(1)} %copy-done, f32[256,128]{1,0:T(8,128)S(1)} %copy-done.1), custom_call_target="tpu_custom_call" | custom-call | tf_op jit(solution)/shard_map/project_out/pallas_call | solution.py:471
  (19 shorter events, 0.2 us)
Async XLA Ops:
  77.1 3.5 %collective-permute-start.30 = (f32[8,392,128]{2,1,0:T(8,128)S(1)}, f32[8,392,128]{2,1,0:T(8,128)S(1)}, u32[]{:S(2)}, u32[]{:S(2)}) collective-permute-start(f32[8,392,128]{2,1,0:T(8,128)S(1)} %get-tuple-element.46), channel_id=1, source_target_pairs={{0,1},{1,0},{2,3},{3,2},{4,5},{5,4},{6,7},{7,6},{8,9},{9,8},{10,11... | collective-permute-start | bytes 4816904 | tf_op jit(solution)/shard_map/cond/branch_2_fun/ppermute | solution.py:488
  77.3 3.3 %collective-permute-start.31 = (f32[8,128]{1,0:T(8,128)S(1)}, f32[8,128]{1,0:T(8,128)S(1)}, u32[]{:S(2)}, u32[]{:S(2)}) collective-permute-start(f32[8,128]{1,0:T(8,128)S(1)} %get-tuple-element.47.top_ref), channel_id=1, source_target_pairs={{0,1},{1,0},{2,3},{3,2},{4,5},{5,4},{6,7},{7,6},{8,9},{9,8},{10,11... | collective-permute-start | bytes 12296 | tf_op jit(solution)/shard_map/cond/branch_2_fun/ppermute | solution.py:488
  82.0 5.2 %collective-permute-start.32 = (s16[25,16,128]{2,1,0:T(8,128)(2,1)S(1)}, s16[25,16,128]{2,1,0:T(8,128)(2,1)S(1)}, u32[]{:S(2)}, u32[]{:S(2)}) collective-permute-start(s16[25,16,128]{2,1,0:T(8,128)(2,1)S(1)} %get-tuple-element.49), channel_id=1, source_target_pairs={{0,2},{1,3},{2,0},{3,1},{4,6},{5,7},{6,4},{7,5},{8,10},{9,11},{10,... | collective-permute-start | bytes 307208 | tf_op jit(solution)/shard_map/cond/branch_2_fun/ppermute | solution.py:488
  82.5 6.3 %collective-permute-start.33 = (s16[25,16,128]{2,1,0:T(8,128)(2,1)S(1)}, s16[25,16,128]{2,1,0:T(8,128)(2,1)S(1)}, u32[]{:S(2)}, u32[]{:S(2)}) collective-permute-start(s16[25,16,128]{2,1,0:T(8,128)(2,1)S(1)} %get-tuple-element.50), channel_id=1, source_target_pairs={{0,4},{1,5},{2,6},{3,7},{4,0},{5,1},{6,2},{7,3},{8,12},{9,13},{10,... | collective-permute-start | bytes 307208 | tf_op jit(solution)/shard_map/cond/branch_2_fun/ppermute | solution.py:488
  82.9 8.4 %collective-permute-start.34 = (s16[25,16,128]{2,1,0:T(8,128)(2,1)S(1)}, s16[25,16,128]{2,1,0:T(8,128)(2,1)S(1)}, u32[]{:S(2)}, u32[]{:S(2)}) collective-permute-start(s16[25,16,128]{2,1,0:T(8,128)(2,1)S(1)} %get-tuple-element.51), channel_id=1, source_target_pairs={{0,6},{1,7},{2,4},{3,5},{4,2},{5,3},{6,0},{7,1},{8,14},{9,15},{10,... | collective-permute-start | bytes 307208 | tf_op jit(solution)/shard_map/cond/branch_2_fun/ppermute | solution.py:488
  84.7 6.5 %collective-permute-start.35 = (s16[25,16,128]{2,1,0:T(8,128)(2,1)S(1)}, s16[25,16,128]{2,1,0:T(8,128)(2,1)S(1)}, u32[]{:S(2)}, u32[]{:S(2)}) collective-permute-start(s16[25,16,128]{2,1,0:T(8,128)(2,1)S(1)} %get-tuple-element.52), channel_id=1, source_target_pairs={{0,8},{1,9},{2,10},{3,11},{4,12},{5,13},{6,14},{7,15},{8,0},{9,1},... | collective-permute-start | bytes 307208 | tf_op jit(solution)/shard_map/cond/branch_2_fun/ppermute | solution.py:488
  85.6 15.3 %collective-permute-start.36 = (s16[25,16,128]{2,1,0:T(8,128)(2,1)S(1)}, s16[25,16,128]{2,1,0:T(8,128)(2,1)S(1)}, u32[]{:S(2)}, u32[]{:S(2)}) collective-permute-start(s16[25,16,128]{2,1,0:T(8,128)(2,1)S(1)} %get-tuple-element.53), channel_id=1, source_target_pairs={{0,10},{1,11},{2,8},{3,9},{4,14},{5,15},{6,12},{7,13},{8,2},{9,3},... | collective-permute-start | bytes 307208 | tf_op jit(solution)/shard_map/cond/branch_2_fun/ppermute | solution.py:488
  87.2 13.7 %collective-permute-start.37 = (s16[25,16,128]{2,1,0:T(8,128)(2,1)S(1)}, s16[25,16,128]{2,1,0:T(8,128)(2,1)S(1)}, u32[]{:S(2)}, u32[]{:S(2)}) collective-permute-start(s16[25,16,128]{2,1,0:T(8,128)(2,1)S(1)} %get-tuple-element.54), channel_id=1, source_target_pairs={{0,12},{1,13},{2,14},{3,15},{4,8},{5,9},{6,10},{7,11},{8,4},{9,5},... | collective-permute-start | bytes 307208 | tf_op jit(solution)/shard_map/cond/branch_2_fun/ppermute | solution.py:488
  88.7 12.2 %collective-permute-start.38 = (s16[25,16,128]{2,1,0:T(8,128)(2,1)S(1)}, s16[25,16,128]{2,1,0:T(8,128)(2,1)S(1)}, u32[]{:S(2)}, u32[]{:S(2)}) collective-permute-start(s16[25,16,128]{2,1,0:T(8,128)(2,1)S(1)} %get-tuple-element.55), channel_id=1, source_target_pairs={{0,14},{1,15},{2,12},{3,13},{4,10},{5,11},{6,8},{7,9},{8,6},{9,7},... | collective-permute-start | bytes 307208 | tf_op jit(solution)/shard_map/cond/branch_2_fun/ppermute | solution.py:488
  102.8 7.3 %collective-permute-start.39 = (bf16[1,25,16,128]{3,2,1,0:T(8,128)(2,1)S(1)}, bf16[1,25,16,128]{3,2,1,0:T(8,128)(2,1)S(1)}, u32[]{:S(2)}, u32[]{:S(2)}) collective-permute-start(bf16[1,25,16,128]{3,2,1,0:T(8,128)(2,1)S(1)} %bitcast.41), channel_id=1, source_target_pairs={{0,8},{1,9},{2,10},{3,11},{4,12},{5,13},{6,14},{7,15},{8,0},{9,1},... | collective-permute-start | bytes 307208 | tf_op jit(solution)/shard_map/cond/branch_2_fun/ppermute | solution.py:488
  110.2 5.3 %collective-permute-start.40 = (bf16[2,25,16,128]{3,2,1,0:T(8,128)(2,1)S(1)}, bf16[2,25,16,128]{3,2,1,0:T(8,128)(2,1)S(1)}, u32[]{:S(2)}, u32[]{:S(2)}) collective-permute-start(bf16[2,25,16,128]{3,2,1,0:T(8,128)(2,1)S(1)} %pad_maximum_fusion.2), channel_id=1, source_target_pairs={{0,4},{1,5},{2,6},{3,7},{4,0},{5,1},{6,2},{7,3},{8,12},{9,13},{10,... | collective-permute-start | bytes 614408 | tf_op jit(solution)/shard_map/cond/branch_2_fun/ppermute | solution.py:488
  112.1 3.6 %collective-permute-start.41 = (bf16[1,25,16,128]{3,2,1,0:T(8,128)(2,1)S(1)}, bf16[1,25,16,128]{3,2,1,0:T(8,128)(2,1)S(1)}, u32[]{:S(2)}, u32[]{:S(2)}) collective-permute-start(bf16[1,25,16,128]{3,2,1,0:T(8,128)(2,1)S(1)} %bitcast.43), channel_id=1, source_target_pairs={{0,2},{1,3},{2,0},{3,1},{4,6},{5,7},{6,4},{7,5},{8,10},{9,11},{10,... | collective-permute-start | bytes 307208 | tf_op jit(solution)/shard_map/cond/branch_2_fun/ppermute | solution.py:488
  112.6 4.2 %collective-permute-start.42 = (bf16[1,25,16,128]{3,2,1,0:T(8,128)(2,1)S(1)}, bf16[1,25,16,128]{3,2,1,0:T(8,128)(2,1)S(1)}, u32[]{:S(2)}, u32[]{:S(2)}) collective-permute-start(bf16[1,25,16,128]{3,2,1,0:T(8,128)(2,1)S(1)} %collective-permute-done.39), channel_id=1, source_target_pairs={{0,2},{1,3},{2,0},{3,1},{4,6},{5,7},{6,4},{7,5},{8,10},{9,11},{10,... | collective-permute-start | bytes 307208 | tf_op jit(solution)/shard_map/cond/branch_2_fun/ppermute | solution.py:488
  115.4 7.0 %collective-permute-start.43 = (bf16[2,25,16,128]{3,2,1,0:T(8,128)(2,1)S(1)}, bf16[2,25,16,128]{3,2,1,0:T(8,128)(2,1)S(1)}, u32[]{:S(2)}, u32[]{:S(2)}) collective-permute-start(bf16[2,25,16,128]{3,2,1,0:T(8,128)(2,1)S(1)} %collective-permute-done.40), channel_id=1, source_target_pairs={{0,2},{1,3},{2,0},{3,1},{4,6},{5,7},{6,4},{7,5},{8,10},{9,11},{10,... | collective-permute-start | bytes 614408 | tf_op jit(solution)/shard_map/cond/branch_2_fun/ppermute | solution.py:488
  122.5 5.9 %collective-permute-start.44 = (bf16[8,25,16,128]{3,2,1,0:T(8,128)(2,1)S(1)}, bf16[8,25,16,128]{3,2,1,0:T(8,128)(2,1)S(1)}, u32[]{:S(2)}, u32[]{:S(2)}) collective-permute-start(bf16[8,25,16,128]{3,2,1,0:T(8,128)(2,1)S(1)} %constant_dynamic-update-slice_fusion.12.refs_0_), channel_id=1, source_target_pairs={{0,1},{1,0},{2,3},{3,2},{4,5},{5,4},{6,7},{7,6},{8,9},{9,8},{10,11... | collective-permute-start | bytes 2457608 | tf_op jit(solution)/shard_map/cond/branch_2_fun/ppermute | solution.py:488
  138.6 51.2 %copy-start = (bf16[256,4096]{1,0:T(8,128)(2,1)S(1)}, bf16[256,4096]{1,0:T(8,128)(2,1)}, u32[]{:S(2)}) copy-start(bf16[256,4096]{1,0:T(8,128)(2,1)} %get-tuple-element.135.normed_ref) | copy-start | bytes 6291460
  138.7 51.2 %copy-start.1 = (f32[256,128]{1,0:T(8,128)S(1)}, f32[256,128]{1,0:T(8,128)}, u32[]{:S(2)}) copy-start(f32[256,128]{1,0:T(8,128)} %get-tuple-element.136.inv_ref) | copy-start | bytes 393220
